TPU v7x, 128 devices: a whole 4x4x4 slice. The times are simulated.
128 devices in a mesh: grp: 64 (over z, y, x), blk: 2 (over core).
Axes of the slice: x: 4, y: 4, z: 4, core: 2. Of those that a mesh axis runs over, the one named last changes fastest.
Arguments:
- embeddings: bfloat16 [131072, 1024], P(('grp', 'blk'))
- labels: int32 [131072], P(('grp', 'blk')), may hold values from 0 to 1023, as said below
- row_ids: int32 [131072], P(('grp', 'blk')), may hold values from 0 to 131071, each once
Outputs:
- best: float32 [131072], P(('grp', 'blk'))
Inputs may be any that keep to these rules, and one draw needn't show every extreme that they name: Cluster c is owned by group c divided by 16, rounded down. In each device's aligned block of 1024 rows, at most 32 labels are of clusters that one group owns, and exactly 32 for some group.
All inputs are finite; a program needn't handle non-finite values.
Results may differ from a plain program's by a relative error of at most 0.0006.
Values may be sent and summed in bfloat16 or wider, within the bound.
No kernel may reach another device: no remote copies, remote signals or barrier semaphores. Data moves between devices by JAX's collectives and lax.ppermute only.
A program may use at most 64 MiB of HBM per device.

v0:
```python
import math

import jax
import jax.numpy as jnp
from jax import lax
from jax.sharding import PartitionSpec as P

CL_GRP = 16


def row_maxima(gram, q_lab, q_ids, k_lab, k_ids):
    mask = (
        (k_lab[None, :] == q_lab[:, None])
        & (k_ids[None, :] < q_ids[:, None])
        & (k_lab[None, :] >= 0)
    )
    return jnp.max(jnp.where(mask, gram, jnp.float32(-1.0)), axis=1)


def inner(left, right):
    return lax.dot_general(
        left, right, (((1,), (1,)), ((), ())), preferred_element_type=jnp.float32
    )


def rows_only(queries, q_lab, q_ids, keys, k_lab, k_ids):
    count = queries.shape[0]
    block = math.gcd(512, count)
    steps = count // block

    def one_block(part):
        q_vec, q_lb, q_id = part
        return row_maxima(inner(q_vec, keys), q_lb, q_id, k_lab, k_ids)

    return lax.map(
        one_block,
        (
            queries.reshape(steps, block, -1),
            q_lab.reshape(steps, block),
            q_ids.reshape(steps, block),
        ),
    ).reshape(count)


def local(embeddings, labels, row_ids):
    groups = lax.axis_size("grp")
    rows = embeddings.shape[0]
    width = embeddings.shape[1]
    per_group = 2 * rows // groups
    wide = embeddings.astype(jnp.float32)
    unit = (wide * lax.rsqrt(jnp.sum(wide * wide, axis=1, keepdims=True) + 1e-06)).astype(
        jnp.bfloat16
    )
    target = labels // CL_GRP
    onehot = (target[:, None] == jnp.arange(groups, dtype=jnp.int32)[None, :]).astype(jnp.int32)
    ranks = jnp.sum(onehot * (jnp.cumsum(onehot, axis=0) - 1), axis=1)
    slot = target * per_group + ranks
    slots_all = groups * per_group
    send_vec = jnp.zeros((slots_all, width), jnp.bfloat16).at[slot].set(unit)
    send_meta = jnp.zeros((slots_all, 2), jnp.int32).at[:, 0].set(-1)
    send_meta = send_meta.at[slot].set(jnp.stack([labels, row_ids], axis=1))
    initial = jnp.full((slots_all,), -1.0, jnp.float32)
    got_vec, got_meta = (
        lax.all_to_all(
            send_vec.reshape(groups, per_group, width),
            "grp",
            split_axis=0,
            concat_axis=0,
            tiled=True,
        ),
        lax.all_to_all(
            send_meta.reshape(groups, per_group, 2), "grp", split_axis=0, concat_axis=0, tiled=True
        ),
    )
    queries = got_vec.reshape(slots_all, width)
    meta = got_meta.reshape(slots_all, 2)
    q_lab = meta[:, 0]
    q_ids = meta[:, 1]
    key_vec = lax.all_gather(queries, "blk", axis=0, tiled=True)
    key_meta = lax.all_gather(meta, "blk", axis=0, tiled=True)
    found = jnp.maximum(
        initial, rows_only(queries, q_lab, q_ids, key_vec, key_meta[:, 0], key_meta[:, 1])
    )
    back = lax.all_to_all(
        found.reshape(groups, per_group), "grp", split_axis=0, concat_axis=0, tiled=True
    )
    return back.reshape(slots_all)[slot]


def solution(mesh):
    in_specs = (P(("grp", "blk"), None), P(("grp", "blk")), P(("grp", "blk")))
    out_specs = P(("grp", "blk"))
    return jax.shard_map(local, mesh=mesh, in_specs=in_specs, out_specs=out_specs, check_vma=False)
```

profile of v0, /device:TPU:1, one launch (start us, length us, event | category | flops | bytes accessed | tf_op | source)
XLA Modules:
  0.0 196.0 jit_solution(395562972443807893)
XLA Ops:
  6.5 0.8 add_select_fusion
  7.4 18.0 %reduce-window.6 = s32[64,8,128]{2,1,0:T(8,128)S(1)} reduce-window(s32[64,8,128]{2,1,0:T(8,128)S(1)} %fusion.11, s32[]{:T(128)} %constant.73.clone.1), window={size=1x1x128 pad=0_0x0_0x127_0}, to_apply=%region_0.0 | reduce-window | flops 8323072 | bytes 524292 | tf_op jit(solution)/shard_map/reduce-window
  25.6 0.1 copy.11
  26.0 0.7 broadcast_clamp_fusion
  26.7 2.1 %fusion.3 = f32[1024]{0:T(1024)S(1)} fusion(bf16[1024,1024]{1,0:T(8,128)(2,1)} %param.7), kind=kLoop, calls=%fused_computation.12 | loop fusion | flops 3144704 | bytes 2101248 | tf_op jit(solution)/shard_map/reduce_sum | solution.py:51
  28.8 8.3 %scatter_custom_fusion.1 = bf16[2048,1024]{1,0:T(8,128)(2,1)} fusion(s32[1024]{0:T(1024)S(1)} %get-tuple-element.79, bf16[1024,1024]{1,0:T(8,128)(2,1)S(1)} %copy-done.1, f32[1024]{0:T(1024)S(1)} %add_rsqrt_fusion, bf16[]{:T(256)} %constant.75.clone.1), kind=kCustom, calls=%fused_computation.14 | custom fusion | flops 3145728 | bytes 6295554 | tf_op jit(solution)/shard_map/scatter | solution.py:59
  37.1 63.0 %all_to_all.16 = bf16[64,32,1024]{2,1,0:T(8,128)(2,1)} all-to-all(bf16[64,32,1024]{2,1,0:T(8,128)(2,1)} %bitcast.51), channel_id=1, replica_groups=mesh['grp'=64,'blk'=2] {'grp'}, dimensions={0} | all-to-all | bytes 8388608 | tf_op jit(solution)/shard_map/all_to_all | solution.py:64
  100.2 0.7 copy-done.2
  100.9 0.2 copy.13
  101.1 0.3 copy-done
  101.4 3.5 %scatter_fusion = s32[2048,2]{1,0:T(8,128)S(1)} fusion(s32[2048,2]{1,0:T(8,128)S(1)} %copy-done, s32[1024]{0:T(1024)S(1)} %get-tuple-element.79, s32[1024,2]{1,0:T(8,128)S(1)} %copy.13), kind=kCustom, calls=%fused_computation.1 | custom fusion | bytes 28672 | tf_op jit(solution)/shard_map/scatter | solution.py:61
  104.9 1.1 copy.15
  106.0 7.7 %all-to-all-start = ((s32[64,32,2]{1,2,0:T(2,128)}), s32[64,32,2]{1,2,0:T(2,128)S(1)}, u32[]{:S(2)}, u32[]{:S(2)}) async-start(s32[64,32,2]{1,2,0:T(2,128)} %copy.15), calls=%async_computation | async-start | bytes 131072 | tf_op jit(solution)/shard_map/all_to_all | solution.py:71
  113.6 8.4 %all-to-all-done = s32[64,32,2]{1,2,0:T(2,128)S(1)} async-done(((s32[64,32,2]{1,2,0:T(2,128)}), s32[64,32,2]{1,2,0:T(2,128)S(1)}, u32[]{:S(2)}, u32[]{:S(2)}) %all-to-all-start) | async-done | bytes 16416 | tf_op jit(solution)/shard_map/all_to_all | solution.py:71
  122.2 3.6 %all_gather.6 = s32[4096,2]{0,1:T(2,128)S(1)} all-gather(s32[2048,2]{0,1:T(2,128)S(1)} %reshape.94), channel_id=1, replica_groups=mesh['grp'=64,'blk'=2] {'blk'}, dimensions={0}, use_global_device_ids=true | all-gather | bytes 49152 | tf_op jit(solution)/shard_map/all_gather | solution.py:80
  125.9 36.9 %while.11 = (s32[]{:T(128)}, f32[4,512]{1,0:T(4,128)S(1)}, s32[4096,1]{0,1:T(1,128)S(1)}, s32[4,512]{1,0:T(4,128)S(1)}, s32[4096,1]{0,1:T(1,128)S(1)}, /*index=5...) while((s32[]{:T(128)}, f32[4,512]{1,0:T(4,128)S(1)}, ...), condition=%wide.region_8.9_spmd, body=%wide.region_6.8_spmd.sunk | while | flops 4307553792 | bytes 9513581 | solution.py:35
  125.9 9.1 %select_reduce_fusion.2 = f32[512]{0:T(512)S(1)} fusion(bf16[4096,1024]{1,0:T(8,128)(2,1)} %get-tuple-element.166, s32[4096]{0:T(1024)S(1)} %bitcast.61, s32[4096]{0:T(1024)S(1)} %bitcast.54, s32[512]{0:T(512)S(1)} %bitcast.56, s32[512]{0:T(512)S(1)} %bitcast.57, pred[4096]{0:T(1024)(128)(4,1)S(1)} %broadcast_compare_fusion.2, ...), kind=kOutput, calls=%fused_computation.3.clone.1 | convolution fusion | flops 4307549696 | bytes 9480704 | tf_op jit(solution)/shard_map/while/body/eval_jaxpr/dot_general | solution.py:21
  135.2 9.1 %select_reduce_fusion.2 = f32[512]{0:T(512)S(1)} fusion(bf16[4096,1024]{1,0:T(8,128)(2,1)} %get-tuple-element.166, s32[4096]{0:T(1024)S(1)} %bitcast.61, s32[4096]{0:T(1024)S(1)} %bitcast.54, s32[512]{0:T(512)S(1)} %bitcast.56, s32[512]{0:T(512)S(1)} %bitcast.57, pred[4096]{0:T(1024)(128)(4,1)S(1)} %broadcast_compare_fusion.2, ...), kind=kOutput, calls=%fused_computation.3.clone.1 | convolution fusion | flops 4307549696 | bytes 9480704 | tf_op jit(solution)/shard_map/while/body/eval_jaxpr/dot_general | solution.py:21
  144.4 9.1 %select_reduce_fusion.2 = f32[512]{0:T(512)S(1)} fusion(bf16[4096,1024]{1,0:T(8,128)(2,1)} %get-tuple-element.166, s32[4096]{0:T(1024)S(1)} %bitcast.61, s32[4096]{0:T(1024)S(1)} %bitcast.54, s32[512]{0:T(512)S(1)} %bitcast.56, s32[512]{0:T(512)S(1)} %bitcast.57, pred[4096]{0:T(1024)(128)(4,1)S(1)} %broadcast_compare_fusion.2, ...), kind=kOutput, calls=%fused_computation.3.clone.1 | convolution fusion | flops 4307549696 | bytes 9480704 | tf_op jit(solution)/shard_map/while/body/eval_jaxpr/dot_general | solution.py:21
  153.6 9.1 %select_reduce_fusion.2 = f32[512]{0:T(512)S(1)} fusion(bf16[4096,1024]{1,0:T(8,128)(2,1)} %get-tuple-element.166, s32[4096]{0:T(1024)S(1)} %bitcast.61, s32[4096]{0:T(1024)S(1)} %bitcast.54, s32[512]{0:T(512)S(1)} %bitcast.56, s32[512]{0:T(512)S(1)} %bitcast.57, pred[4096]{0:T(1024)(128)(4,1)S(1)} %broadcast_compare_fusion.2, ...), kind=kOutput, calls=%fused_computation.3.clone.1 | convolution fusion | flops 4307549696 | bytes 9480704 | tf_op jit(solution)/shard_map/while/body/eval_jaxpr/dot_general | solution.py:21
  162.9 14.5 %all_to_all.17 = f32[64,1,32]{2,1,0:T(1,128)S(1)} all-to-all(f32[64,1,32]{2,1,0:T(1,128)S(1)} %bitcast.55), channel_id=1, replica_groups=mesh['grp'=64,'blk'=2] {'grp'}, dimensions={0} | all-to-all | bytes 16384 | tf_op jit(solution)/shard_map/all_to_all | solution.py:84
  177.3 0.5 broadcast.115
  177.9 0.7 reduce.13
  178.7 10.5 %gather_fusion = f32[1024]{0:T(1024)} fusion(f32[2048]{0:T(1024)S(1)} %reshape.97, s32[1024]{0:T(1024)S(1)} %get-tuple-element.78), kind=kCustom, calls=%fused_computation | custom fusion | bytes 12288 | tf_op jit(solution)/shard_map/gather | solution.py:87
  (40 shorter events, 1.1 us)
Async XLA Ops:
  6.5 22.3 %copy-start.1 = (bf16[1024,1024]{1,0:T(8,128)(2,1)S(1)}, bf16[1024,1024]{1,0:T(8,128)(2,1)}, u32[]{:S(2)}) copy-start(bf16[1024,1024]{1,0:T(8,128)(2,1)} %param.7) | copy-start | bytes 6291460
  6.5 119.4 %all-gather.2.cloned.1.call-start = ((), (), s32[]{:S(2)}) async-start(), calls=%async_computation.3 | async-start | bytes 12582912 | tf_op jit(solution)/shard_map/all_gather | solution.py:79
  100.2 0.7 copy-start.2
  100.2 0.7 copy-start.3
  100.2 1.3 copy-start
  106.0 16.1 %all-to-all-start = ((s32[64,32,2]{1,2,0:T(2,128)}), s32[64,32,2]{1,2,0:T(2,128)S(1)}, u32[]{:S(2)}, u32[]{:S(2)}) async-start(s32[64,32,2]{1,2,0:T(2,128)} %copy.15), calls=%async_computation | async-start | bytes 131072 | tf_op jit(solution)/shard_map/all_to_all | solution.py:71
Sparse Core Ops, SparseCore 0:
  100.3 21.7 all-gather.1
where the time goes:
time: 197 us; the launch traced here: 196 us
  blocking collectives  81.1 us (41%)
  matrix products  36.5 us (19%)
  other arithmetic  30.9 us (16%)
  local copies, waits for them, and re-layouts  17.7 us (9%)
  between operations  13.5 us (7%)
  waiting for transfers between devices  8.46 us (4%)
  starting transfers between devices  7.66 us (4%)
    all_to_all x1, blocking collectives, local(): lax.all_to_all(send_vec.reshape(groups, per_group, width), 'grp', split_a...  63 us
    dot_general x4, matrix products, inner(): lax.dot_general(left, right, (((1,), (1,)), ((), ())), preferred_element_...  36.5 us
    another operation x2, other arithmetic  18 us
    all_to_all x1, blocking collectives, local(): lax.all_to_all(found.reshape(groups, per_group), 'grp', split_axis=0, con...  14.5 us
    gather x1, local copies, waits for them, and re-layouts, local(): return back.reshape(slots_all)[slot]  10.5 us
    all_to_all x1, waiting for transfers between devices, local(): lax.all_to_all(send_meta.reshape(groups, per_group, 2), 'grp', split_axis...  8.42 us
    scatter x1, other arithmetic, local(): send_vec = jnp.zeros((slots_all, width), jnp.bfloat16).at[slot].set(unit)  8.29 us
    all_to_all x1, starting transfers between devices, local(): lax.all_to_all(send_meta.reshape(groups, per_group, 2), 'grp', split_axis...  7.66 us
  transfers between devices with their start and end apart: 2, of which 1 were waited for; matrix products, arithmetic and copies ran while one was open for 3% of the time, Pallas kernels for 0%

commit v1 on v0

v1 whole, which is shorter than its diff:
```python
import functools

import jax
import jax.numpy as jnp
from jax import lax
from jax.experimental import pallas as pl
from jax.experimental.pallas import tpu as pltpu
from jax.sharding import PartitionSpec as P

CAP = 32
CL_GRP = 16
LANES = 128
NT = (((1,), (1,)), ((), ()))


def pack_kernel(groups, labels_ref, ids_ref, emb_ref, out_ref, slot_ref, raw, unit, slots, meta, sems):
    step = pl.program_id(0)
    block = out_ref.shape[0]
    rows, width = unit.shape
    lines = rows // LANES
    parts = sems.shape[0]
    part = rows // parts

    def copy(p):
        span = pl.ds(p * part, part)
        return pltpu.make_async_copy(emb_ref.at[span], raw.at[span], sems.at[p])

    @pl.when(step == 0)
    def _():
        for p in range(parts):
            copy(p).start()
        labels = labels_ref[...]
        place = (
            lax.broadcasted_iota(jnp.int32, (lines, LANES), 0) * LANES
            + lax.broadcasted_iota(jnp.int32, (lines, LANES), 1)
        )
        key = (labels * rows + place).astype(jnp.float32)
        target = lax.shift_right_logical(labels, 4)
        low = (target * (CL_GRP * rows)).astype(jnp.float32)
        tall = jnp.concatenate([key, jnp.zeros((LANES - lines, LANES), jnp.float32)], axis=0).T

        def flat(x):
            return jnp.concatenate([x[b : b + 1] for b in range(lines)], axis=1)

        key_row, low_row = flat(key), flat(low)
        count = jnp.zeros((LANES, rows), jnp.float32)
        for b in range(lines):
            col = tall[:, b : b + 1]
            count += jnp.where((col >= low_row) & (col < key_row), 1.0, 0.0)
        rank = jnp.sum(count, axis=0, keepdims=True)
        slot = flat(target * CAP) + rank.astype(jnp.int32)
        slots[...] = slot
        slot_ref[...] = slot
        ids = ids_ref[...]
        first = flat((ids & 255).astype(jnp.float32))
        second = flat((lax.shift_right_logical(ids, 8) & 255).astype(jnp.float32))
        third = flat(
            ((labels & (CL_GRP - 1)) * 2 + lax.shift_right_logical(ids, 16) + 1).astype(jnp.float32)
        )
        meta[...] = jnp.concatenate(
            [first, second, third, jnp.zeros((meta.shape[0] - 3, rows), jnp.float32)], axis=0
        ).astype(jnp.bfloat16)
        for p in range(parts):
            copy(p).wait()
            wide = raw[p * part : (p + 1) * part].astype(jnp.float32)
            scale = lax.rsqrt(jnp.sum(wide * wide, axis=1, keepdims=True) + 1e-06)
            unit[p * part : (p + 1) * part] = (wide * scale).astype(jnp.bfloat16)

    span = block * CAP
    base = step * span
    wanted = lax.broadcasted_iota(jnp.int32, (span, rows), 0) + base
    pick = jnp.where(slots[...] == wanted, 1.0, 0.0).astype(jnp.bfloat16)
    packed = jnp.dot(pick, unit[...], preferred_element_type=jnp.float32).astype(jnp.bfloat16)
    for j in range(width // LANES):
        out_ref[:, j * CAP : (j + 1) * CAP, :] = packed[:, j * LANES : (j + 1) * LANES].reshape(
            block, CAP, LANES
        )
    tags = lax.dot_general(meta[...], pick, NT, preferred_element_type=jnp.float32)
    tail = width // LANES * CAP
    for g in range(block):
        at = g * CAP // LANES * LANES
        line = tags[:8, at : at + LANES]
        turn = g * CAP % LANES
        if turn:
            line = pltpu.roll(line, LANES - turn, 1)
        out_ref[g, tail : tail + 8, :] = line.astype(jnp.bfloat16)


def pack(embeddings, labels, row_ids, groups):
    rows, width = embeddings.shape
    lines = rows // LANES
    depth = width // LANES * CAP + 8
    block = 16
    parts = 4
    return pl.pallas_call(
        functools.partial(pack_kernel, groups),
        grid=(groups // block,),
        in_specs=[
            pl.BlockSpec((lines, LANES), lambda i: (0, 0)),
            pl.BlockSpec((lines, LANES), lambda i: (0, 0)),
            pl.BlockSpec(memory_space=pl.ANY),
        ],
        out_specs=[
            pl.BlockSpec((block, depth, LANES), lambda i: (i, 0, 0)),
            pl.BlockSpec((1, rows), lambda i: (0, 0)),
        ],
        out_shape=[
            jax.ShapeDtypeStruct((groups, depth, LANES), jnp.bfloat16),
            jax.ShapeDtypeStruct((1, rows), jnp.int32),
        ],
        scratch_shapes=[
            pltpu.VMEM((rows, width), jnp.bfloat16),
            pltpu.VMEM((rows, width), jnp.bfloat16),
            pltpu.VMEM((1, rows), jnp.int32),
            pltpu.VMEM((16, rows), jnp.bfloat16),
            pltpu.SemaphoreType.DMA((parts,)),
        ],
        compiler_params=pltpu.CompilerParams(vmem_limit_bytes=48 << 20),
        cost_estimate=pl.CostEstimate(
            flops=2 * groups * CAP * rows * width, bytes_accessed=6 * rows * width, transcendentals=rows
        ),
    )(labels.reshape(lines, LANES), row_ids.reshape(lines, LANES), embeddings)


def codes(block):
    tags = block.astype(jnp.float32)
    return (tags[:, 2, :] - 1.0) * 65536.0 + tags[:, 1, :] * 256.0 + tags[:, 0, :]


def gram_kernel(q_ref, k_ref, prev_ref, out_ref, vecs, order, q_code, q_low, acc):
    step = pl.program_id(0)
    senders = q_ref.shape[0]
    chunks = vecs.shape[1] // LANES
    tail = chunks * CAP
    block = k_ref.shape[0]
    per = LANES // CAP
    lines = senders // per
    lane = lax.broadcasted_iota(jnp.int32, (lines, LANES), 1)

    @pl.when(step == 0)
    def _():
        for j in range(chunks):
            vecs[:, j * LANES : (j + 1) * LANES] = q_ref[:, j * CAP : (j + 1) * CAP, :].reshape(
                senders * CAP, LANES
            )
        order[...] = codes(q_ref[:, tail : tail + 8, :])
        code = order[pl.ds(0, lines, stride=per), :]
        for k in range(1, per):
            code = jnp.where(
                lane >= k * CAP, pltpu.roll(order[pl.ds(k, lines, stride=per), :], k * CAP, 1), code
            )
        low = jnp.floor(code * (1.0 / 131072.0)) * 131072.0
        for t in range(lines):
            q_code[:, t * LANES : (t + 1) * LANES] = code[t : t + 1]
            q_low[:, t * LANES : (t + 1) * LANES] = low[t : t + 1]
        acc[...] = jnp.full(acc.shape, -1.0, jnp.float32)

    keys = jnp.concatenate(
        [
            k_ref[:, j * CAP : (j + 1) * CAP, :].reshape(block * CAP, LANES)
            for j in range(chunks)
        ],
        axis=1,
    )
    k_code = codes(k_ref[:, tail : tail + 8, :])
    tall = jnp.concatenate([k_code, jnp.zeros((LANES - block, LANES), jnp.float32)], axis=0).T
    col = jnp.concatenate([tall[:CAP, s : s + 1] for s in range(block)], axis=0)
    wide = 512
    for c in range(senders * CAP // wide):
        span = slice(c * wide, (c + 1) * wide)
        score = lax.dot_general(keys, vecs[span], NT, preferred_element_type=jnp.float32)
        seen = (col >= q_low[:, span]) & (col < q_code[:, span])
        score = jnp.where(seen, score, -1.0)
        acc[:, span] = jnp.maximum(
            acc[:, span], jnp.max(score.reshape(block * CAP // 8, 8, wide), axis=0)
        )

    @pl.when(step == pl.num_programs(0) - 1)
    def _():
        best = jnp.max(acc[...], axis=0, keepdims=True)
        best = jnp.concatenate([best[:, t * LANES : (t + 1) * LANES] for t in range(lines)], axis=0)
        for k in range(per):
            turned = pltpu.roll(best, LANES - k * CAP, 1) if k else best
            order[pl.ds(k, lines, stride=per), :] = turned
        out_ref[...] = jnp.maximum(prev_ref[...], order[...])


def gram(queries, keys, prev):
    senders, depth, _ = queries.shape
    chunks = depth // CAP
    block = 8
    count = senders * CAP
    return pl.pallas_call(
        gram_kernel,
        grid=(senders // block,),
        in_specs=[
            pl.BlockSpec((senders, depth, LANES), lambda i: (0, 0, 0)),
            pl.BlockSpec((block, depth, LANES), lambda i: (i, 0, 0)),
            pl.BlockSpec((senders, LANES), lambda i: (0, 0)),
        ],
        out_specs=pl.BlockSpec((senders, LANES), lambda i: (0, 0)),
        out_shape=jax.ShapeDtypeStruct((senders, LANES), jnp.float32),
        scratch_shapes=[
            pltpu.VMEM((count, chunks * LANES), jnp.bfloat16),
            pltpu.VMEM((senders, LANES), jnp.float32),
            pltpu.VMEM((1, count), jnp.float32),
            pltpu.VMEM((1, count), jnp.float32),
            pltpu.VMEM((8, count), jnp.float32),
        ],
        compiler_params=pltpu.CompilerParams(vmem_limit_bytes=48 << 20),
        cost_estimate=pl.CostEstimate(
            flops=2 * count * count * chunks * LANES,
            bytes_accessed=4 * count * chunks * LANES,
            transcendentals=0,
        ),
    )(queries, keys, prev)


def unpack_kernel(back_ref, slot_ref, out_ref):
    groups = back_ref.shape[0]
    rows = slot_ref.shape[1]
    slot = slot_ref[...]
    group = lax.shift_right_logical(slot, 5)
    rank = slot & (CAP - 1)
    member = lax.broadcasted_iota(jnp.int32, (groups, rows), 0) == group
    member = jnp.where(member, 1.0, 0.0).astype(jnp.bfloat16)
    rest = back_ref[...]
    found = jnp.zeros((LANES, rows), jnp.float32)
    for _ in range(3):
        piece = rest.astype(jnp.bfloat16)
        rest = rest - piece.astype(jnp.float32)
        found += lax.dot_general(
            piece, member, (((0,), (0,)), ((), ())), preferred_element_type=jnp.float32
        )
    chosen = lax.broadcasted_iota(jnp.int32, (CAP, rows), 0) == rank
    best = jnp.sum(jnp.where(chosen, found[:CAP], 0.0), axis=0, keepdims=True)
    out_ref[...] = jnp.concatenate(
        [best[:, b * LANES : (b + 1) * LANES] for b in range(rows // LANES)], axis=0
    )


def unpack(back, slot):
    rows = slot.shape[1]
    return pl.pallas_call(
        unpack_kernel,
        out_shape=jax.ShapeDtypeStruct((rows // LANES, LANES), jnp.float32),
    )(back, slot)


def local(embeddings, labels, row_ids):
    groups = lax.axis_size("grp")
    rows = embeddings.shape[0]
    send, slot = pack(embeddings, labels, row_ids, groups)
    own = lax.all_to_all(send, "grp", split_axis=0, concat_axis=0, tiled=True)
    other = lax.ppermute(own, "blk", [(0, 1), (1, 0)])
    found = jnp.full((groups, LANES), -1.0, jnp.float32)
    found = gram(own, own, found)
    found = gram(own, other, found)
    back = lax.all_to_all(found, "grp", split_axis=0, concat_axis=0, tiled=True)
    return unpack(back, slot).reshape(rows)


def solution(mesh):
    in_specs = (P(("grp", "blk"), None), P(("grp", "blk")), P(("grp", "blk")))
    out_specs = P(("grp", "blk"))
    return jax.shard_map(local, mesh=mesh, in_specs=in_specs, out_specs=out_specs, check_vma=False)
```

time: 197 us -> 126 us (0.64)
  Pallas kernels: 0 us -> 39.5 us
  matrix products: 36.5 us -> 0 us
  other arithmetic: 30.9 us -> 0 us
  between operations: 13.5 us -> 0.03 us
  local copies, waits for them, and re-layouts: 17.7 us -> 4.96 us
  waiting for transfers between devices: 8.46 us -> 0.01 us
  starting transfers between devices: 7.66 us -> 1.94 us
  blocking collectives: 81.1 us -> 78.8 us
    pallas_call x0 -> x4, Pallas kernels: none -> 39.5 us  [the longest x2 28.8 us: gram(): pl.pallas_call(gram_kernel, grid=(senders // block,), in_specs=[pl.BlockS...]
    dot_general x4 -> x0, matrix products: 36.5 us -> none  [inner(): lax.dot_general(left, right, (((1,), (1,)), ((), ())), preferred_element_...]
    another operation x4 -> x0, other arithmetic: 18.1 us -> none
    gather x1 -> x0, local copies, waits for them, and re-layouts: 10.5 us -> none  [local(): return back.reshape(slots_all)[slot]]
    all_to_all x1 -> x0, waiting for transfers between devices: 8.42 us -> none  [local(): lax.all_to_all(send_meta.reshape(groups, per_group, 2), 'grp', split_axis...]
    scatter x1 -> x0, other arithmetic: 8.29 us -> none  [local(): send_vec = jnp.zeros((slots_all, width), jnp.bfloat16).at[slot].set(unit)]
    all_to_all x1 -> x0, starting transfers between devices: 7.66 us -> none  [local(): lax.all_to_all(send_meta.reshape(groups, per_group, 2), 'grp', split_axis...]
    unnamed x8 -> x10, local copies, waits for them, and re-layouts: 0.99 us -> 4.95 us
  transfers between devices with their start and end apart: 2 -> 1, of which waited for: 1 -> 0; matrix products, arithmetic and copies ran while one was open for 3% -> 0% of each run, Pallas kernels for 0% -> 11%
where the time goes in v1:
time: 126 us; the launch traced here: 125 us
  blocking collectives  78.8 us (63%)
  Pallas kernels  39.5 us (31%)
  local copies, waits for them, and re-layouts  4.96 us (4%)
  starting transfers between devices  1.94 us (2%)
    all_to_all x1, blocking collectives, local(): own = lax.all_to_all(send, 'grp', split_axis=0, concat_axis=0, tiled=True)  65.1 us
    pallas_call x2, Pallas kernels, gram(): pl.pallas_call(gram_kernel, grid=(senders // block,), in_specs=[pl.BlockS...  28.8 us
    all_to_all x1, blocking collectives, local(): back = lax.all_to_all(found, 'grp', split_axis=0, concat_axis=0, tiled=True)  13.6 us
    pallas_call x1, Pallas kernels, pack(): pl.pallas_call(functools.partial(pack_kernel, groups), grid=(groups // bl...  8.92 us
    unnamed x10, local copies, waits for them, and re-layouts  4.95 us
  transfers between devices with their start and end apart: 1, of which 0 were waited for; matrix products, arithmetic and copies ran while one was open for 0% of the time, Pallas kernels for 11%

profile of v1, /device:TPU:1, one launch (start us, length us, event | category | flops | bytes accessed | tf_op | source)
XLA Modules:
  0.0 125.2 jit_solution(17165160728484870552)
XLA Ops:
  0.0 0.0 copy-start.1
  0.0 1.6 %copy-done.1 = bf16[1024,1024]{1,0:T(8,128)(2,1)S(1)} copy-done((bf16[1024,1024]{1,0:T(8,128)(2,1)S(1)}, bf16[1024,1024]{1,0:T(8,128)(2,1)}, u32[]{:S(2)}) %copy-start.1) | copy-done | bytes 2097176
  1.6 0.0 copy-start.2
  1.6 0.7 copy-done.2
  2.3 0.0 copy-start.3
  2.3 0.7 copy-done.3
  3.0 8.9 %shard_map.37 = (bf16[64,264,128]{2,1,0:T(8,128)(2,1)}, s32[1,1024]{1,0:T(1,128)S(1)}) custom-call(s32[8,128]{1,0:T(8,128)S(1)} %bitcast.8, s32[8,128]{1,0:T(8,128)S(1)} %bitcast.9, bf16[1024,1024]{1,0:T(8,128)(2,1)S(1)} %copy-done.1), custom_call_target="tpu_custom_call" | custom-call | flops 4294967296 | bytes 6291456 | tf_op jit(solution)/shard_map/pallas_call | solution.py:95
  11.9 0.0 copy-start
  11.9 65.1 %all_to_all.16.q_ref.k_ref = bf16[64,264,128]{2,1,0:T(8,128)(2,1)S(1)} all-to-all(bf16[64,264,128]{2,1,0:T(8,128)(2,1)} %get-tuple-element.7), channel_id=1, replica_groups=mesh['grp'=64,'blk'=2] {'grp'}, dimensions={0} | all-to-all | bytes 8650752 | tf_op jit(solution)/shard_map/all_to_all | solution.py:254
  77.0 0.0 copy-done
  77.0 1.9 %collective-permute-start = (bf16[64,264,128]{2,1,0:T(8,128)(2,1)S(1)}, bf16[64,264,128]{2,1,0:T(8,128)(2,1)S(1)}, u32[]{:S(2)}, u32[]{:S(2)}) collective-permute-start(bf16[64,264,128]{2,1,0:T(8,128)(2,1)S(1)} %all_to_all.16.q_ref.k_ref), channel_id=1, source_target_pairs={{0,1},{1,0},{2,3},{3,2},{4,5},{5,4},{6,7},{7,6},{8,9},{9,8},{10,11... | collective-permute-start | bytes 12976136 | tf_op jit(solution)/shard_map/ppermute | solution.py:255
  79.0 13.9 %shard_map.38.prev_ref = f32[64,128]{1,0:T(8,128)S(1)} custom-call(bf16[64,264,128]{2,1,0:T(8,128)(2,1)S(1)} %all_to_all.16.q_ref.k_ref, bf16[64,264,128]{2,1,0:T(8,128)(2,1)S(1)} %all_to_all.16.q_ref.k_ref, f32[64,128]{1,0:T(8,128)S(1)} %broadcast_in_dim.3.prev_ref), custom_call_target="tpu_custom_call" | custom-call | flops 8589934592 | bytes 8388608 | tf_op jit(solution)/shard_map/pallas_call | solution.py:193
  92.9 0.0 collective-permute-done.k_ref
  92.9 0.0 copy-start.4
  92.9 2.0 %copy-done.4 = bf16[64,264,128]{2,1,0:T(8,128)(2,1)} copy-done((bf16[64,264,128]{2,1,0:T(8,128)(2,1)}, bf16[64,264,128]{2,1,0:T(8,128)(2,1)S(1)}, u32[]{:S(2)}) %copy-start.4) | copy-done | bytes 4325400
  94.9 15.0 %shard_map.39 = f32[64,128]{1,0:T(8,128)S(1)} custom-call(bf16[64,264,128]{2,1,0:T(8,128)(2,1)S(1)} %all_to_all.16.q_ref.k_ref, bf16[64,264,128]{2,1,0:T(8,128)(2,1)} %copy-done.4, f32[64,128]{1,0:T(8,128)S(1)} %shard_map.38.prev_ref), custom_call_target="tpu_custom_call" | custom-call | flops 8589934592 | bytes 8388608 | tf_op jit(solution)/shard_map/pallas_call | solution.py:193
  109.8 13.6 %all_to_all.17 = f32[64,1,128]{2,1,0:T(1,128)} all-to-all(f32[64,1,128]{2,1,0:T(1,128)S(1)} %bitcast.7), channel_id=1, replica_groups=mesh['grp'=64,'blk'=2] {'grp'}, dimensions={0} | all-to-all | bytes 65536 | tf_op jit(solution)/shard_map/all_to_all | solution.py:259
  123.4 1.7 %shard_map.40 = f32[8,128]{1,0:T(8,128)} custom-call(f32[64,128]{1,0:T(8,128)} %bitcast.10, s32[1,1024]{1,0:T(1,128)} %copy-done), custom_call_target="tpu_custom_call" | custom-call | tf_op jit(solution)/shard_map/pallas_call | solution.py:244
  (1 shorter events, 0.0 us)
Async XLA Ops:
  0.0 1.6 %copy-start.1 = (bf16[1024,1024]{1,0:T(8,128)(2,1)S(1)}, bf16[1024,1024]{1,0:T(8,128)(2,1)}, u32[]{:S(2)}) copy-start(bf16[1024,1024]{1,0:T(8,128)(2,1)} %emb_ref.1) | copy-start | bytes 6291460
  1.6 0.7 copy-start.2
  2.3 0.7 copy-start.3
  11.9 65.2 %copy-start = (s32[1,1024]{1,0:T(1,128)}, s32[1,1024]{1,0:T(1,128)S(1)}, u32[]{:S(2)}) copy-start(s32[1,1024]{1,0:T(1,128)S(1)} %get-tuple-element.8.slot_ref) | copy-start | bytes 12292
  77.0 15.8 %collective-permute-start = (bf16[64,264,128]{2,1,0:T(8,128)(2,1)S(1)}, bf16[64,264,128]{2,1,0:T(8,128)(2,1)S(1)}, u32[]{:S(2)}, u32[]{:S(2)}) collective-permute-start(bf16[64,264,128]{2,1,0:T(8,128)(2,1)S(1)} %all_to_all.16.q_ref.k_ref), channel_id=1, source_target_pairs={{0,1},{1,0},{2,3},{3,2},{4,5},{5,4},{6,7},{7,6},{8,9},{9,8},{10,11... | collective-permute-start | bytes 12976136 | tf_op jit(solution)/shard_map/ppermute | solution.py:255
  92.9 2.0 %copy-start.4 = (bf16[64,264,128]{2,1,0:T(8,128)(2,1)}, bf16[64,264,128]{2,1,0:T(8,128)(2,1)S(1)}, u32[]{:S(2)}) copy-start(bf16[64,264,128]{2,1,0:T(8,128)(2,1)S(1)} %collective-permute-done.k_ref) | copy-start | bytes 12976132

commit v2 on v1

--- a/solution.py
+++ b/solution.py
@@ -115,7 +115,7 @@
             pltpu.VMEM((16, rows), jnp.bfloat16),
             pltpu.SemaphoreType.DMA((parts,)),
         ],
-        compiler_params=pltpu.CompilerParams(vmem_limit_bytes=48 << 20),
+        compiler_params=pltpu.CompilerParams(vmem_limit_bytes=62 << 20),
         cost_estimate=pl.CostEstimate(
             flops=2 * groups * CAP * rows * width, bytes_accessed=6 * rows * width, transcendentals=rows
         ),
@@ -127,87 +127,90 @@
     return (tags[:, 2, :] - 1.0) * 65536.0 + tags[:, 1, :] * 256.0 + tags[:, 0, :]
 
 
-def gram_kernel(q_ref, k_ref, prev_ref, out_ref, vecs, order, q_code, q_low, acc):
-    step = pl.program_id(0)
-    senders = q_ref.shape[0]
-    chunks = vecs.shape[1] // LANES
-    tail = chunks * CAP
-    block = k_ref.shape[0]
+def rows_of(ref, sender, count):
+    chunks = ref.shape[1] // CAP
+    return jnp.concatenate(
+        [
+            ref[sender : sender + count, j * CAP : (j + 1) * CAP, :].reshape(count * CAP, LANES)
+            for j in range(chunks)
+        ],
+        axis=1,
+    )
+
+
+def gram_kernel(q_ref, k_ref, prev_ref, out_ref, order, q_code, q_low, k_code, acc, *scores):
+    senders, depth, _ = q_ref.shape
+    tail = depth // CAP * CAP
     per = LANES // CAP
     lines = senders // per
     lane = lax.broadcasted_iota(jnp.int32, (lines, LANES), 1)
-
-    @pl.when(step == 0)
-    def _():
-        for j in range(chunks):
-            vecs[:, j * LANES : (j + 1) * LANES] = q_ref[:, j * CAP : (j + 1) * CAP, :].reshape(
-                senders * CAP, LANES
-            )
-        order[...] = codes(q_ref[:, tail : tail + 8, :])
-        code = order[pl.ds(0, lines, stride=per), :]
-        for k in range(1, per):
-            code = jnp.where(
-                lane >= k * CAP, pltpu.roll(order[pl.ds(k, lines, stride=per), :], k * CAP, 1), code
-            )
-        low = jnp.floor(code * (1.0 / 131072.0)) * 131072.0
-        for t in range(lines):
-            q_code[:, t * LANES : (t + 1) * LANES] = code[t : t + 1]
-            q_low[:, t * LANES : (t + 1) * LANES] = low[t : t + 1]
-        acc[...] = jnp.full(acc.shape, -1.0, jnp.float32)
-
-    keys = jnp.concatenate(
-        [
-            k_ref[:, j * CAP : (j + 1) * CAP, :].reshape(block * CAP, LANES)
-            for j in range(chunks)
-        ],
-        axis=1,
-    )
-    k_code = codes(k_ref[:, tail : tail + 8, :])
-    tall = jnp.concatenate([k_code, jnp.zeros((LANES - block, LANES), jnp.float32)], axis=0).T
-    col = jnp.concatenate([tall[:CAP, s : s + 1] for s in range(block)], axis=0)
-    wide = 512
-    for c in range(senders * CAP // wide):
-        span = slice(c * wide, (c + 1) * wide)
-        score = lax.dot_general(keys, vecs[span], NT, preferred_element_type=jnp.float32)
-        seen = (col >= q_low[:, span]) & (col < q_code[:, span])
-        score = jnp.where(seen, score, -1.0)
-        acc[:, span] = jnp.maximum(
-            acc[:, span], jnp.max(score.reshape(block * CAP // 8, 8, wide), axis=0)
-        )
-
-    @pl.when(step == pl.num_programs(0) - 1)
-    def _():
-        best = jnp.max(acc[...], axis=0, keepdims=True)
-        best = jnp.concatenate([best[:, t * LANES : (t + 1) * LANES] for t in range(lines)], axis=0)
-        for k in range(per):
-            turned = pltpu.roll(best, LANES - k * CAP, 1) if k else best
-            order[pl.ds(k, lines, stride=per), :] = turned
-        out_ref[...] = jnp.maximum(prev_ref[...], order[...])
+    order[...] = codes(q_ref[:, tail : tail + 8, :])
+    code = order[pl.ds(0, lines, stride=per), :]
+    for k in range(1, per):
+        code = jnp.where(
+            lane >= k * CAP, pltpu.roll(order[pl.ds(k, lines, stride=per), :], k * CAP, 1), code
+        )
+    low = jnp.floor(code * (1.0 / 131072.0)) * 131072.0
+    for t in range(lines):
+        q_code[:, t * LANES : (t + 1) * LANES] = code[t : t + 1]
+        q_low[:, t * LANES : (t + 1) * LANES] = low[t : t + 1]
+    tall = codes(k_ref[:, tail : tail + 8, :])
+    tall = jnp.concatenate([tall, jnp.zeros((LANES - senders, LANES), jnp.float32)], axis=0).T
+    for s in range(senders):
+        k_code[s * CAP : (s + 1) * CAP, :] = jnp.broadcast_to(tall[:CAP, s : s + 1], (CAP, LANES))
+    acc[...] = jnp.full(acc.shape, -1.0, jnp.float32)
+
+    def reduce_tile(at, k0, q0):
+        score = scores[at]
+        size, wide = score.shape
+        for c in range(0, wide, LANES):
+            span = slice(q0 + c, q0 + c + LANES)
+            col = k_code[k0 : k0 + size, :]
+            seen = (col >= q_low[:, span]) & (col < q_code[:, span])
+            part = jnp.where(seen, score[:, c : c + LANES], -1.0).reshape(size // 8, 8, LANES)
+            acc[:, span] = jnp.maximum(acc[:, span], jnp.max(part, axis=0))
+
+    size, wide = scores[0].shape
+    tiles = [(k0, q0) for k0 in range(0, senders * CAP, size) for q0 in range(0, senders * CAP, wide)]
+    for n, (k0, q0) in enumerate(tiles):
+        scores[n % 2][...] = lax.dot_general(
+            rows_of(k_ref, k0 // CAP, size // CAP),
+            rows_of(q_ref, q0 // CAP, wide // CAP),
+            NT,
+            preferred_element_type=jnp.float32,
+        )
+        if n:
+            reduce_tile((n - 1) % 2, *tiles[n - 1])
+    reduce_tile((len(tiles) - 1) % 2, *tiles[-1])
+
+    best = jnp.max(acc[...], axis=0, keepdims=True)
+    best = jnp.concatenate([best[:, t * LANES : (t + 1) * LANES] for t in range(lines)], axis=0)
+    for k in range(per):
+        order[pl.ds(k, lines, stride=per), :] = pltpu.roll(best, LANES - k * CAP, 1) if k else best
+    out_ref[...] = jnp.maximum(prev_ref[...], order[...])
 
 
 def gram(queries, keys, prev):
     senders, depth, _ = queries.shape
     chunks = depth // CAP
-    block = 8
     count = senders * CAP
+    tile = min(1024, count)
+    here = pl.BlockSpec(memory_space=pltpu.VMEM)
     return pl.pallas_call(
         gram_kernel,
-        grid=(senders // block,),
-        in_specs=[
-            pl.BlockSpec((senders, depth, LANES), lambda i: (0, 0, 0)),
-            pl.BlockSpec((block, depth, LANES), lambda i: (i, 0, 0)),
-            pl.BlockSpec((senders, LANES), lambda i: (0, 0)),
-        ],
-        out_specs=pl.BlockSpec((senders, LANES), lambda i: (0, 0)),
+        in_specs=[here] * 3,
+        out_specs=here,
         out_shape=jax.ShapeDtypeStruct((senders, LANES), jnp.float32),
         scratch_shapes=[
-            pltpu.VMEM((count, chunks * LANES), jnp.bfloat16),
             pltpu.VMEM((senders, LANES), jnp.float32),
             pltpu.VMEM((1, count), jnp.float32),
             pltpu.VMEM((1, count), jnp.float32),
+            pltpu.VMEM((count, LANES), jnp.float32),
             pltpu.VMEM((8, count), jnp.float32),
-        ],
-        compiler_params=pltpu.CompilerParams(vmem_limit_bytes=48 << 20),
+            pltpu.VMEM((tile, tile), jnp.float32),
+            pltpu.VMEM((tile, tile), jnp.float32),
+        ],
+        compiler_params=pltpu.CompilerParams(vmem_limit_bytes=24 << 20),
         cost_estimate=pl.CostEstimate(
             flops=2 * count * count * chunks * LANES,
             bytes_accessed=4 * count * chunks * LANES,

time: 126 us -> 113 us (0.90)
  Pallas kernels: 39.5 us -> 31.7 us
  local copies, waits for them, and re-layouts: 4.96 us -> 0.01 us
    pallas_call x2, Pallas kernels: 28.8 us -> 20.3 us  [gram(): pl.pallas_call(gram_kernel, in_specs=[here] * 3, out_specs=here, out_shap...]
    unnamed x10 -> x0, local copies, waits for them, and re-layouts: 4.95 us -> none
  transfers between devices with their start and end apart: 1 -> 1, of which waited for: 0 -> 0; matrix products, arithmetic and copies ran while one was open for 0% -> 0% of each run, Pallas kernels for 11% -> 9%
where the time goes in v2:
time: 113 us; the launch traced here: 112 us
  blocking collectives  78.7 us (70%)
  Pallas kernels  31.7 us (28%)
  starting transfers between devices  1.92 us (2%)
    all_to_all x1, blocking collectives, local(): own = lax.all_to_all(send, 'grp', split_axis=0, concat_axis=0, tiled=True)  65.2 us
    pallas_call x2, Pallas kernels, gram(): pl.pallas_call(gram_kernel, in_specs=[here] * 3, out_specs=here, out_shap...  20.3 us
    all_to_all x1, blocking collectives, local(): back = lax.all_to_all(found, 'grp', split_axis=0, concat_axis=0, tiled=True)  13.5 us
    pallas_call x1, Pallas kernels, pack(): pl.pallas_call(functools.partial(pack_kernel, groups), grid=(groups // bl...  9.67 us
  transfers between devices with their start and end apart: 1, of which 0 were waited for; matrix products, arithmetic and copies ran while one was open for 0% of the time, Pallas kernels for 9%

profile of v2, /device:TPU:1, one launch (start us, length us, event | category | flops | bytes accessed | tf_op | source)
XLA Modules:
  0.0 112.3 jit_solution(17501376642995720624)
XLA Ops:
  0.0 9.7 %shard_map.37 = (bf16[64,264,128]{2,1,0:T(8,128)(2,1)}, s32[1,1024]{1,0:T(1,128)}) custom-call(s32[8,128]{1,0:T(8,128)} %bitcast.9, s32[8,128]{1,0:T(8,128)} %bitcast.10, bf16[1024,1024]{1,0:T(8,128)(2,1)} %emb_ref.1), custom_call_target="tpu_custom_call" | custom-call | flops 4294967296 | bytes 6291456 | tf_op jit(solution)/shard_map/pallas_call | solution.py:95
  9.7 65.2 %all_to_all.16.q_ref.k_ref = bf16[64,264,128]{2,1,0:T(8,128)(2,1)S(1)} all-to-all(bf16[64,264,128]{2,1,0:T(8,128)(2,1)} %get-tuple-element.7), channel_id=1, replica_groups=mesh['grp'=64,'blk'=2] {'grp'}, dimensions={0} | all-to-all | bytes 8650752 | tf_op jit(solution)/shard_map/all_to_all | solution.py:257
  74.9 1.9 %collective-permute-start = (bf16[64,264,128]{2,1,0:T(8,128)(2,1)S(1)}, bf16[64,264,128]{2,1,0:T(8,128)(2,1)S(1)}, u32[]{:S(2)}, u32[]{:S(2)}) collective-permute-start(bf16[64,264,128]{2,1,0:T(8,128)(2,1)S(1)} %all_to_all.16.q_ref.k_ref), channel_id=1, source_target_pairs={{0,1},{1,0},{2,3},{3,2},{4,5},{5,4},{6,7},{7,6},{8,9},{9,8},{10,11... | collective-permute-start | bytes 12976136 | tf_op jit(solution)/shard_map/ppermute | solution.py:258
  76.8 10.1 %shard_map.38.prev_ref = f32[64,128]{1,0:T(8,128)S(1)} custom-call(bf16[64,264,128]{2,1,0:T(8,128)(2,1)S(1)} %all_to_all.16.q_ref.k_ref, bf16[64,264,128]{2,1,0:T(8,128)(2,1)S(1)} %all_to_all.16.q_ref.k_ref, f32[64,128]{1,0:T(8,128)S(1)} %broadcast_in_dim.3.prev_ref), custom_call_target="tpu_custom_call" | custom-call | flops 8589934592 | bytes 8388608 | tf_op jit(solution)/shard_map/pallas_call | solution.py:199
  86.9 0.0 collective-permute-done.k_ref
  86.9 10.2 %shard_map.39 = f32[64,128]{1,0:T(8,128)S(1)} custom-call(bf16[64,264,128]{2,1,0:T(8,128)(2,1)S(1)} %all_to_all.16.q_ref.k_ref, bf16[64,264,128]{2,1,0:T(8,128)(2,1)S(1)} %collective-permute-done.k_ref, f32[64,128]{1,0:T(8,128)S(1)} %shard_map.38.prev_ref), custom_call_target="tpu_custom_call" | custom-call | flops 8589934592 | bytes 8388608 | tf_op jit(solution)/shard_map/pallas_call | solution.py:199
  97.1 13.5 %all_to_all.17 = f32[64,1,128]{2,1,0:T(1,128)} all-to-all(f32[64,1,128]{2,1,0:T(1,128)S(1)} %bitcast.7), channel_id=1, replica_groups=mesh['grp'=64,'blk'=2] {'grp'}, dimensions={0} | all-to-all | bytes 65536 | tf_op jit(solution)/shard_map/all_to_all | solution.py:262
  110.6 1.7 %shard_map.40 = f32[8,128]{1,0:T(8,128)} custom-call(f32[64,128]{1,0:T(8,128)} %bitcast.8, s32[1,1024]{1,0:T(1,128)} %get-tuple-element.8.slot_ref), custom_call_target="tpu_custom_call" | custom-call | tf_op jit(solution)/shard_map/pallas_call | solution.py:247
  (1 shorter events, 0.0 us)
Async XLA Ops:
  74.9 12.1 %collective-permute-start = (bf16[64,264,128]{2,1,0:T(8,128)(2,1)S(1)}, bf16[64,264,128]{2,1,0:T(8,128)(2,1)S(1)}, u32[]{:S(2)}, u32[]{:S(2)}) collective-permute-start(bf16[64,264,128]{2,1,0:T(8,128)(2,1)S(1)} %all_to_all.16.q_ref.k_ref), channel_id=1, source_target_pairs={{0,1},{1,0},{2,3},{3,2},{4,5},{5,4},{6,7},{7,6},{8,9},{9,8},{10,11... | collective-permute-start | bytes 12976136 | tf_op jit(solution)/shard_map/ppermute | solution.py:258

commit v3 on v2

--- a/solution.py
+++ b/solution.py
@@ -127,99 +127,227 @@
     return (tags[:, 2, :] - 1.0) * 65536.0 + tags[:, 1, :] * 256.0 + tags[:, 0, :]
 
 
+def low_of(code):
+    return jnp.floor(code * (1.0 / 131072.0)) * 131072.0
+
+
+def code_lines(ref, order):
+    senders, depth, _ = ref.shape
+    tail = depth // CAP * CAP
+    per = LANES // CAP
+    lines = senders // per
+    lane = lax.broadcasted_iota(jnp.int32, (lines, LANES), 1)
+    order[...] = codes(ref[:, tail : tail + 8, :])
+    code = order[pl.ds(0, lines, stride=per), :]
+    for k in range(1, per):
+        turned = pltpu.roll(order[pl.ds(k, lines, stride=per), :], k * CAP, 1)
+        code = jnp.where(lane >= k * CAP, turned, code)
+    return code
+
+
+def code_columns(ref, col_code, col_low):
+    senders, depth, _ = ref.shape
+    tail = depth // CAP * CAP
+    tall = codes(ref[:, tail : tail + 8, :])
+    tall = jnp.concatenate([tall, jnp.zeros((LANES - senders, LANES), jnp.float32)], axis=0).T
+    for s in range(senders):
+        col = jnp.broadcast_to(tall[:CAP, s : s + 1], (CAP, LANES))
+        col_code[s * CAP : (s + 1) * CAP, :] = col
+        col_low[s * CAP : (s + 1) * CAP, :] = low_of(col)
+
+
 def rows_of(ref, sender, count):
     chunks = ref.shape[1] // CAP
     return jnp.concatenate(
         [
-            ref[sender : sender + count, j * CAP : (j + 1) * CAP, :].reshape(count * CAP, LANES)
+            ref[pl.ds(sender, count), j * CAP : (j + 1) * CAP, :].reshape(count * CAP, LANES)
             for j in range(chunks)
         ],
         axis=1,
     )
 
 
-def gram_kernel(q_ref, k_ref, prev_ref, out_ref, order, q_code, q_low, k_code, acc, *scores):
-    senders, depth, _ = q_ref.shape
-    tail = depth // CAP * CAP
+def reduce_tile(score, wide, row0, col_code, col_low, col_best, lanes):
+    size = score.shape[0]
+    step = 64
+    tops = [None] * (wide // LANES)
+    for r in range(0, size, step):
+        rows = slice(row0 + r, row0 + r + step)
+        code, low = col_code[rows, :], col_low[rows, :]
+        side = None
+        for c, (lane_code, lane_low, _, _, both) in enumerate(lanes):
+            here = score[r : r + step, c * LANES : (c + 1) * LANES]
+            here = jnp.where(low == lane_low, here, -1.0)
+            less = code < lane_code
+            top = jnp.max(jnp.where(less, here, -1.0).reshape(step // 8, 8, LANES), axis=0)
+            tops[c] = top if tops[c] is None else jnp.maximum(tops[c], top)
+            if both:
+                late = jnp.where(less, -1.0, here)
+                side = late if side is None else jnp.maximum(side, late)
+        if side is not None:
+            col_best[rows, :] = jnp.maximum(col_best[rows, :], side)
+    for top, (_, _, read, write, _) in zip(tops, lanes):
+        write(jnp.maximum(read(), top))
+
+
+def column_maxima(col_best):
+    lines = col_best.shape[0] // LANES
+    return jnp.concatenate(
+        [
+            jnp.max(col_best[t * LANES : (t + 1) * LANES, :].T, axis=0, keepdims=True)
+            for t in range(lines)
+        ],
+        axis=0,
+    )
+
+
+def own_kernel(own_ref, out_ref, order, lane_code, lane_low, col_code, col_low, col_best, best, *scores):
+    senders = own_ref.shape[0]
+    count = senders * CAP
+    size, most = scores[0].shape
+    code = code_lines(own_ref, order)
+    low = low_of(code)
+    for t in range(count // LANES):
+        lane_code[:, t * LANES : (t + 1) * LANES] = code[t : t + 1]
+        lane_low[:, t * LANES : (t + 1) * LANES] = low[t : t + 1]
+    code_columns(own_ref, col_code, col_low)
+    col_best[...] = jnp.full(col_best.shape, -1.0, jnp.float32)
+    best[...] = jnp.full(best.shape, -1.0, jnp.float32)
+
+    def reduce(at, r0, c0, wide):
+        lanes = []
+        for c in range(c0, c0 + wide, LANES):
+            span = slice(c, c + LANES)
+
+            def read(span=span):
+                return best[:, span]
+
+            def write(x, span=span):
+                best[:, span] = x
+
+            lanes.append((lane_code[:, span], lane_low[:, span], read, write, c >= r0 + size))
+        reduce_tile(scores[at], wide, r0, col_code, col_low, col_best, lanes)
+
+    tiles = [
+        (r0, c0, min(most, count - c0)) for r0 in range(0, count, size) for c0 in range(r0, count, most)
+    ]
+    for n, (r0, c0, wide) in enumerate(tiles):
+        scores[n % 2][:, :wide] = lax.dot_general(
+            rows_of(own_ref, r0 // CAP, size // CAP),
+            rows_of(own_ref, c0 // CAP, wide // CAP),
+            NT,
+            preferred_element_type=jnp.float32,
+        )
+        if n:
+            reduce((n - 1) % 2, *tiles[n - 1])
+    reduce((len(tiles) - 1) % 2, *tiles[-1])
+    top = jnp.max(best[...], axis=0, keepdims=True)
+    top = jnp.concatenate([top[:, t : t + LANES] for t in range(0, count, LANES)], axis=0)
+    out_ref[...] = jnp.maximum(top, column_maxima(col_best))
+
+
+def cross_kernel(
+    own_ref, other_ref, prev_ref, out_ref, order, lane_code, lane_low, col_code, col_low, col_best, best, *scores
+):
+    senders = own_ref.shape[0]
+    count = senders * CAP
+    size, most = scores[0].shape
+    blocks = count // size
+    each = size // LANES
+    core = lax.axis_index("blk")
+    code = code_lines(other_ref, order)
+    low = low_of(code)
+    for t in range(count // LANES):
+        span = slice(t % each * LANES, (t % each + 1) * LANES)
+        lane_code[t // each : t // each + 1, span] = code[t : t + 1]
+        lane_low[t // each : t // each + 1, span] = low[t : t + 1]
+    code_columns(own_ref, col_code, col_low)
+    col_best[...] = jnp.full(col_best.shape, -1.0, jnp.float32)
+    best[...] = jnp.full(best.shape, -1.0, jnp.float32)
+
+    def others(n):
+        return [lax.rem(n + core + k, blocks) for k in range(blocks // 2)]
+
+    def reduce(n):
+        lanes = []
+        for j in others(n):
+            code_here, low_here = lane_code[pl.ds(j, 1), :], lane_low[pl.ds(j, 1), :]
+            for c in range(0, size, LANES):
+                span = slice(c, c + LANES)
+
+                def read(j=j, span=span):
+                    return best[j, :, span]
+
+                def write(x, j=j, span=span):
+                    best[j, :, span] = x
+
+                lanes.append((code_here[:, span], low_here[:, span], read, write, True))
+        reduce_tile(scores[n % 2], most, n * size, col_code, col_low, col_best, lanes)
+
+    for n in range(blocks):
+        scores[n % 2][...] = lax.dot_general(
+            rows_of(own_ref, n * size // CAP, size // CAP),
+            jnp.concatenate(
+                [rows_of(other_ref, j * (size // CAP), size // CAP) for j in others(n)], axis=0
+            ),
+            NT,
+            preferred_element_type=jnp.float32,
+        )
+        if n:
+            reduce(n - 1)
+    reduce(blocks - 1)
+
     per = LANES // CAP
     lines = senders // per
+    mine = jnp.maximum(prev_ref[...], column_maxima(col_best))
+    theirs = jnp.concatenate(
+        [
+            jnp.max(best[t // each, :, t % each * LANES : (t % each + 1) * LANES], axis=0, keepdims=True)
+            for t in range(lines)
+        ],
+        axis=0,
+    )
     lane = lax.broadcasted_iota(jnp.int32, (lines, LANES), 1)
-    order[...] = codes(q_ref[:, tail : tail + 8, :])
-    code = order[pl.ds(0, lines, stride=per), :]
-    for k in range(1, per):
-        code = jnp.where(
-            lane >= k * CAP, pltpu.roll(order[pl.ds(k, lines, stride=per), :], k * CAP, 1), code
-        )
-    low = jnp.floor(code * (1.0 / 131072.0)) * 131072.0
-    for t in range(lines):
-        q_code[:, t * LANES : (t + 1) * LANES] = code[t : t + 1]
-        q_low[:, t * LANES : (t + 1) * LANES] = low[t : t + 1]
-    tall = codes(k_ref[:, tail : tail + 8, :])
-    tall = jnp.concatenate([tall, jnp.zeros((LANES - senders, LANES), jnp.float32)], axis=0).T
-    for s in range(senders):
-        k_code[s * CAP : (s + 1) * CAP, :] = jnp.broadcast_to(tall[:CAP, s : s + 1], (CAP, LANES))
-    acc[...] = jnp.full(acc.shape, -1.0, jnp.float32)
-
-    def reduce_tile(at, k0, q0):
-        score = scores[at]
-        size, wide = score.shape
-        for c in range(0, wide, LANES):
-            span = slice(q0 + c, q0 + c + LANES)
-            col = k_code[k0 : k0 + size, :]
-            seen = (col >= q_low[:, span]) & (col < q_code[:, span])
-            part = jnp.where(seen, score[:, c : c + LANES], -1.0).reshape(size // 8, 8, LANES)
-            acc[:, span] = jnp.maximum(acc[:, span], jnp.max(part, axis=0))
-
-    size, wide = scores[0].shape
-    tiles = [(k0, q0) for k0 in range(0, senders * CAP, size) for q0 in range(0, senders * CAP, wide)]
-    for n, (k0, q0) in enumerate(tiles):
-        scores[n % 2][...] = lax.dot_general(
-            rows_of(k_ref, k0 // CAP, size // CAP),
-            rows_of(q_ref, q0 // CAP, wide // CAP),
-            NT,
-            preferred_element_type=jnp.float32,
-        )
-        if n:
-            reduce_tile((n - 1) % 2, *tiles[n - 1])
-    reduce_tile((len(tiles) - 1) % 2, *tiles[-1])
-
-    best = jnp.max(acc[...], axis=0, keepdims=True)
-    best = jnp.concatenate([best[:, t * LANES : (t + 1) * LANES] for t in range(lines)], axis=0)
     for k in range(per):
-        order[pl.ds(k, lines, stride=per), :] = pltpu.roll(best, LANES - k * CAP, 1) if k else best
-    out_ref[...] = jnp.maximum(prev_ref[...], order[...])
-
-
-def gram(queries, keys, prev):
-    senders, depth, _ = queries.shape
-    chunks = depth // CAP
+        first = pltpu.roll(mine, (LANES - k * CAP) % LANES, 1) if k else mine
+        second = pltpu.roll(theirs, (LANES + CAP - k * CAP) % LANES, 1) if k != 1 else theirs
+        order[pl.ds(k, lines, stride=per), :] = jnp.where(lane < CAP, first, second)
+    out_ref[...] = order[...]
+
+
+def gram_call(kernel, out_shape, operands, blocked, senders, depth, pairs):
     count = senders * CAP
-    tile = min(1024, count)
+    size = min(512, count)
+    most = min(1024, count)
     here = pl.BlockSpec(memory_space=pltpu.VMEM)
+    lanes = (count // size, size) if blocked else (1, count)
+    tops = (count // size, 8, size) if blocked else (8, count)
     return pl.pallas_call(
-        gram_kernel,
-        in_specs=[here] * 3,
+        kernel,
+        in_specs=[here] * len(operands),
         out_specs=here,
-        out_shape=jax.ShapeDtypeStruct((senders, LANES), jnp.float32),
+        out_shape=jax.ShapeDtypeStruct(out_shape, jnp.float32),
         scratch_shapes=[
             pltpu.VMEM((senders, LANES), jnp.float32),
-            pltpu.VMEM((1, count), jnp.float32),
-            pltpu.VMEM((1, count), jnp.float32),
+            pltpu.VMEM(lanes, jnp.float32),
+            pltpu.VMEM(lanes, jnp.float32),
             pltpu.VMEM((count, LANES), jnp.float32),
-            pltpu.VMEM((8, count), jnp.float32),
-            pltpu.VMEM((tile, tile), jnp.float32),
-            pltpu.VMEM((tile, tile), jnp.float32),
+            pltpu.VMEM((count, LANES), jnp.float32),
+            pltpu.VMEM((count, LANES), jnp.float32),
+            pltpu.VMEM(tops, jnp.float32),
+            pltpu.VMEM((size, most), jnp.float32),
+            pltpu.VMEM((size, most), jnp.float32),
         ],
         compiler_params=pltpu.CompilerParams(vmem_limit_bytes=24 << 20),
         cost_estimate=pl.CostEstimate(
-            flops=2 * count * count * chunks * LANES,
-            bytes_accessed=4 * count * chunks * LANES,
+            flops=2 * pairs * (depth // CAP) * LANES,
+            bytes_accessed=4 * count * (depth // CAP) * LANES,
             transcendentals=0,
         ),
-    )(queries, keys, prev)
-
-
-def unpack_kernel(back_ref, slot_ref, out_ref):
+    )(*operands)
+
+
+def unpack_kernel(back_ref, swap_ref, slot_ref, out_ref):
     groups = back_ref.shape[0]
     rows = slot_ref.shape[1]
     slot = slot_ref[...]
@@ -227,7 +355,7 @@
     rank = slot & (CAP - 1)
     member = lax.broadcasted_iota(jnp.int32, (groups, rows), 0) == group
     member = jnp.where(member, 1.0, 0.0).astype(jnp.bfloat16)
-    rest = back_ref[...]
+    rest = jnp.maximum(back_ref[...], pltpu.roll(swap_ref[...], LANES - CAP, 1))
     found = jnp.zeros((LANES, rows), jnp.float32)
     for _ in range(3):
         piece = rest.astype(jnp.bfloat16)
@@ -242,12 +370,13 @@
     )
 
 
-def unpack(back, slot):
+def unpack(back, swap, slot):
     rows = slot.shape[1]
     return pl.pallas_call(
         unpack_kernel,
         out_shape=jax.ShapeDtypeStruct((rows // LANES, LANES), jnp.float32),
-    )(back, slot)
+        compiler_params=pltpu.CompilerParams(vmem_limit_bytes=16 << 20),
+    )(back, swap, slot)
 
 
 def local(embeddings, labels, row_ids):
@@ -255,12 +384,18 @@
     rows = embeddings.shape[0]
     send, slot = pack(embeddings, labels, row_ids, groups)
     own = lax.all_to_all(send, "grp", split_axis=0, concat_axis=0, tiled=True)
-    other = lax.ppermute(own, "blk", [(0, 1), (1, 0)])
-    found = jnp.full((groups, LANES), -1.0, jnp.float32)
-    found = gram(own, own, found)
-    found = gram(own, other, found)
+    swap = [(0, 1), (1, 0)]
+    other = lax.ppermute(own, "blk", swap)
+    depth = own.shape[1]
+    count = groups * CAP
+    found = gram_call(
+        own_kernel, (count // LANES, LANES), [own], False, groups, depth, count * count * 5 // 8
+    )
+    found = gram_call(
+        cross_kernel, (groups, LANES), [own, other, found], True, groups, depth, count * count // 2
+    )
     back = lax.all_to_all(found, "grp", split_axis=0, concat_axis=0, tiled=True)
-    return unpack(back, slot).reshape(rows)
+    return unpack(back, lax.ppermute(back, "blk", swap), slot).reshape(rows)
 
 
 def solution(mesh):

time: 113 us -> 107 us (0.947)
  Pallas kernels: 31.7 us -> 23.4 us
  starting transfers between devices: 1.92 us -> 3.53 us
    pallas_call x2, Pallas kernels: 20.3 us -> 12.7 us  [gram_call(): pl.pallas_call(kernel, in_specs=[here] * len(operands), out_specs=here, o...]
    ppermute x1 -> x2, starting transfers between devices: 1.92 us -> 3.53 us  [the longest x1 1.92 us: local(): other = lax.ppermute(own, 'blk', swap)]
  transfers between devices with their start and end apart: 1 -> 2, of which waited for: 0 -> 1; matrix products, arithmetic and copies ran while one was open for 0% -> 0% of each run, Pallas kernels for 9% -> 7%
where the time goes in v3:
time: 107 us; the launch traced here: 106 us
  blocking collectives  78.6 us (73%)
  Pallas kernels  23.4 us (22%)
  starting transfers between devices  3.53 us (3%)
    all_to_all x1, blocking collectives, local(): own = lax.all_to_all(send, 'grp', split_axis=0, concat_axis=0, tiled=True)  65.2 us
    all_to_all x1, blocking collectives, local(): back = lax.all_to_all(found, 'grp', split_axis=0, concat_axis=0, tiled=True)  13.4 us
    pallas_call x2, Pallas kernels, gram_call(): pl.pallas_call(kernel, in_specs=[here] * len(operands), out_specs=here, o...  12.7 us
    pallas_call x1, Pallas kernels, pack(): pl.pallas_call(functools.partial(pack_kernel, groups), grid=(groups // bl...  9.68 us
  transfers between devices with their start and end apart: 2, of which 1 were waited for; matrix products, arithmetic and copies ran while one was open for 0% of the time, Pallas kernels for 7%

profile of v3, /device:TPU:1, one launch (start us, length us, event | category | flops | bytes accessed | tf_op | source)
XLA Modules:
  0.0 106.4 jit_solution(10668864851665773386)
XLA Ops:
  0.0 9.7 %shard_map.37 = (bf16[64,264,128]{2,1,0:T(8,128)(2,1)}, s32[1,1024]{1,0:T(1,128)}) custom-call(s32[8,128]{1,0:T(8,128)} %bitcast.10, s32[8,128]{1,0:T(8,128)} %bitcast.11, bf16[1024,1024]{1,0:T(8,128)(2,1)} %emb_ref.1), custom_call_target="tpu_custom_call" | custom-call | flops 4294967296 | bytes 6291456 | tf_op jit(solution)/shard_map/pallas_call | solution.py:95
  9.7 65.2 %all_to_all.16.own_ref = bf16[64,264,128]{2,1,0:T(8,128)(2,1)S(1)} all-to-all(bf16[64,264,128]{2,1,0:T(8,128)(2,1)} %get-tuple-element.7), channel_id=1, replica_groups=mesh['grp'=64,'blk'=2] {'grp'}, dimensions={0} | all-to-all | bytes 8650752 | tf_op jit(solution)/shard_map/all_to_all | solution.py:386
  74.9 1.9 %collective-permute-start = (bf16[64,264,128]{2,1,0:T(8,128)(2,1)S(1)}, bf16[64,264,128]{2,1,0:T(8,128)(2,1)S(1)}, u32[]{:S(2)}, u32[]{:S(2)}) collective-permute-start(bf16[64,264,128]{2,1,0:T(8,128)(2,1)S(1)} %all_to_all.16.own_ref), channel_id=1, source_target_pairs={{0,1},{1,0},{2,3},{3,2},{4,5},{5,4},{6,7},{7,6},{8,9},{9,8},{10,11... | collective-permute-start | bytes 12976136 | tf_op jit(solution)/shard_map/ppermute | solution.py:388
  76.8 7.1 %shard_map.38.prev_ref = f32[16,128]{1,0:T(8,128)S(1)} custom-call(bf16[64,264,128]{2,1,0:T(8,128)(2,1)S(1)} %all_to_all.16.own_ref), custom_call_target="tpu_custom_call" | custom-call | flops 5368709120 | bytes 8388608 | tf_op jit(solution)/shard_map/pallas_call | solution.py:325
  83.9 0.0 copy-start
  83.9 0.0 collective-permute-done.other_ref
  84.0 5.6 %shard_map.39 = f32[64,128]{1,0:T(8,128)S(1)} custom-call(bf16[64,264,128]{2,1,0:T(8,128)(2,1)S(1)} %all_to_all.16.own_ref, bf16[64,264,128]{2,1,0:T(8,128)(2,1)S(1)} %collective-permute-done.other_ref, f32[16,128]{1,0:T(8,128)S(1)} %shard_map.38.prev_ref), custom_call_target="tpu_custom_call" | custom-call | flops 4294967296 | bytes 8388608 | tf_op jit(solution)/shard_map/pallas_call | solution.py:325
  89.5 13.4 %all_to_all.17 = f32[64,1,128]{2,1,0:T(1,128)S(1)} all-to-all(f32[64,1,128]{2,1,0:T(1,128)S(1)} %bitcast.9), channel_id=1, replica_groups=mesh['grp'=64,'blk'=2] {'grp'}, dimensions={0} | all-to-all | bytes 65536 | tf_op jit(solution)/shard_map/all_to_all | solution.py:397
  102.9 1.6 %collective-permute-start.1 = (f32[64,128]{1,0:T(8,128)S(1)}, f32[64,128]{1,0:T(8,128)S(1)}, u32[]{:S(2)}, u32[]{:S(2)}) collective-permute-start(f32[64,128]{1,0:T(8,128)S(1)} %bitcast.7), channel_id=1, source_target_pairs={{0,1},{1,0},{2,3},{3,2},{4,5},{5,4},{6,7},{7,6},{8,9},{9,8},{10,11... | collective-permute-start | bytes 98312 | tf_op jit(solution)/shard_map/ppermute | solution.py:398
  104.5 0.9 collective-permute-done.1.swap_ref
  105.4 0.0 copy-done
  105.4 1.0 shard_map.40
Async XLA Ops:
  74.9 9.1 %collective-permute-start = (bf16[64,264,128]{2,1,0:T(8,128)(2,1)S(1)}, bf16[64,264,128]{2,1,0:T(8,128)(2,1)S(1)}, u32[]{:S(2)}, u32[]{:S(2)}) collective-permute-start(bf16[64,264,128]{2,1,0:T(8,128)(2,1)S(1)} %all_to_all.16.own_ref), channel_id=1, source_target_pairs={{0,1},{1,0},{2,3},{3,2},{4,5},{5,4},{6,7},{7,6},{8,9},{9,8},{10,11... | collective-permute-start | bytes 12976136 | tf_op jit(solution)/shard_map/ppermute | solution.py:388
  83.9 21.5 %copy-start = (s32[1,1024]{1,0:T(1,128)S(1)}, s32[1,1024]{1,0:T(1,128)}, u32[]{:S(2)}) copy-start(s32[1,1024]{1,0:T(1,128)} %get-tuple-element.8.slot_ref) | copy-start | bytes 12292
  102.9 2.5 %collective-permute-start.1 = (f32[64,128]{1,0:T(8,128)S(1)}, f32[64,128]{1,0:T(8,128)S(1)}, u32[]{:S(2)}, u32[]{:S(2)}) collective-permute-start(f32[64,128]{1,0:T(8,128)S(1)} %bitcast.7), channel_id=1, source_target_pairs={{0,1},{1,0},{2,3},{3,2},{4,5},{5,4},{6,7},{7,6},{8,9},{9,8},{10,11... | collective-permute-start | bytes 98312 | tf_op jit(solution)/shard_map/ppermute | solution.py:398

commit v4 on v3

v4 whole, which is shorter than its diff:
```python
import functools

import jax
import jax.numpy as jnp
from jax import lax
from jax.experimental import pallas as pl
from jax.experimental.pallas import tpu as pltpu
from jax.sharding import PartitionSpec as P

CAP = 32
CL_GRP = 16
LANES = 128
PACK_ENDS = (4, 8, 12, 14, 16)
NT = (((1,), (1,)), ((), ()))


def pack_kernel(
    labels_ref, ids_ref, emb_ref, out_ref, slot_ref, lab, num, raw, unit, stage, slots, first, second, in_sems, out_sems, sems
):
    rows, width = unit.shape
    groups = out_ref.shape[0]
    lines = rows // LANES
    parts, blocks = in_sems.shape[0], out_sems.shape[0]
    part = rows // parts
    ends = [groups * n // 16 for n in PACK_ENDS]
    spans = list(zip([0] + ends[:-1], ends))
    fetch_labels = pltpu.make_async_copy(labels_ref, lab, sems.at[0])
    fetch_ids = pltpu.make_async_copy(ids_ref, num, sems.at[1])
    keep_slots = pltpu.make_async_copy(slots, slot_ref, sems.at[2])
    tail = width // LANES * CAP

    def load(p):
        span = pl.ds(p * part, part)
        return pltpu.make_async_copy(emb_ref.at[span], raw.at[span], in_sems.at[p])

    def store(n):
        span = pl.ds(spans[n][0], spans[n][1] - spans[n][0])
        return pltpu.make_async_copy(stage.at[span], out_ref.at[span], out_sems.at[n])

    fetch_labels.start()
    fetch_ids.start()
    for p in range(parts):
        load(p).start()

    fetch_labels.wait()
    labels = lab[...]
    place = (
        lax.broadcasted_iota(jnp.int32, (lines, LANES), 0) * LANES
        + lax.broadcasted_iota(jnp.int32, (lines, LANES), 1)
    )
    key = (labels * rows + place).astype(jnp.float32)
    target = lax.shift_right_logical(labels, 4)
    low = (target * (CL_GRP * rows)).astype(jnp.float32)
    tall = jnp.concatenate([key, jnp.zeros((LANES - lines, LANES), jnp.float32)], axis=0).T

    def flat(x):
        return jnp.concatenate([x[b : b + 1] for b in range(lines)], axis=1)

    key_row, low_row = flat(key), flat(low)
    count = jnp.zeros((LANES, rows), jnp.float32)
    for b in range(lines):
        col = tall[:, b : b + 1]
        count += jnp.where((col >= low_row) & (col < key_row), 1.0, 0.0)
    rank = jnp.sum(count, axis=0, keepdims=True).astype(jnp.int32)
    group = flat(target)
    slot = group * CAP + rank
    slots[...] = slot
    keep_slots.start()

    fetch_ids.wait()
    ids = num[...]
    pieces = [
        ids & 255,
        lax.shift_right_logical(ids, 8) & 255,
        (labels & (CL_GRP - 1)) * 2 + lax.shift_right_logical(ids, 16) + 1,
    ]
    ranked = lax.broadcasted_iota(jnp.int32, (CAP, rows), 0) == rank
    tags = [jnp.where(ranked, flat(x).astype(jnp.float32), 0.0) for x in pieces]
    tags.append(jnp.zeros((LANES - CAP * len(pieces), rows), jnp.float32))
    tags = jnp.concatenate(tags, axis=0).astype(jnp.bfloat16)
    member = lax.broadcasted_iota(jnp.int32, (LANES, rows), 0) == group
    member = jnp.where(member, 1.0, 0.0).astype(jnp.bfloat16)
    tags = lax.dot_general(member, tags, NT, preferred_element_type=jnp.float32)[:groups]
    stage[:, tail : tail + 8, :] = jnp.broadcast_to(
        tags.reshape(groups, 1, LANES), (groups, 8, LANES)
    ).astype(jnp.bfloat16)

    for p in range(parts):
        load(p).wait()
        wide = raw[p * part : (p + 1) * part].astype(jnp.float32)
        scale = lax.rsqrt(jnp.sum(wide * wide, axis=1, keepdims=True) + 1e-06)
        unit[p * part : (p + 1) * part] = (wide * scale).astype(jnp.bfloat16)

    sums = (first, second)

    def finish(n):
        at, end = spans[n]
        packed = sums[n % 2][: (end - at) * CAP].astype(jnp.bfloat16)
        for j in range(width // LANES):
            stage[at:end, j * CAP : (j + 1) * CAP, :] = packed[
                :, j * LANES : (j + 1) * LANES
            ].reshape(end - at, CAP, LANES)
        store(n).start()

    for n, (at, end) in enumerate(spans):
        size = (end - at) * CAP
        wanted = lax.broadcasted_iota(jnp.int32, (size, rows), 0) + at * CAP
        pick = jnp.where(slot == wanted, 1.0, 0.0).astype(jnp.bfloat16)
        sums[n % 2][:size] = jnp.dot(pick, unit[...], preferred_element_type=jnp.float32)
        if n:
            finish(n - 1)
    finish(blocks - 1)
    for n in range(blocks):
        store(n).wait()
    keep_slots.wait()


def pack(embeddings, labels, row_ids, groups):
    rows, width = embeddings.shape
    lines = rows // LANES
    depth = width // LANES * CAP + 8
    parts, blocks = 4, len(PACK_ENDS)
    there = pl.BlockSpec(memory_space=pl.ANY)
    return pl.pallas_call(
        pack_kernel,
        in_specs=[there] * 3,
        out_specs=[there] * 2,
        out_shape=[
            jax.ShapeDtypeStruct((groups, depth, LANES), jnp.bfloat16),
            jax.ShapeDtypeStruct((1, rows), jnp.int32),
        ],
        scratch_shapes=[
            pltpu.VMEM((lines, LANES), jnp.int32),
            pltpu.VMEM((lines, LANES), jnp.int32),
            pltpu.VMEM((rows, width), jnp.bfloat16),
            pltpu.VMEM((rows, width), jnp.bfloat16),
            pltpu.VMEM((groups, depth, LANES), jnp.bfloat16),
            pltpu.VMEM((1, rows), jnp.int32),
            pltpu.VMEM((groups // 2 * CAP, width), jnp.float32),
            pltpu.VMEM((groups // 2 * CAP, width), jnp.float32),
            pltpu.SemaphoreType.DMA((parts,)),
            pltpu.SemaphoreType.DMA((blocks,)),
            pltpu.SemaphoreType.DMA((3,)),
        ],
        compiler_params=pltpu.CompilerParams(vmem_limit_bytes=62 << 20),
        cost_estimate=pl.CostEstimate(
            flops=2 * groups * CAP * rows * width, bytes_accessed=6 * rows * width, transcendentals=rows
        ),
    )(labels.reshape(lines, LANES), row_ids.reshape(lines, LANES), embeddings)


def codes(block):
    tags = block.astype(jnp.float32)[:, 0, :]
    second, third = pltpu.roll(tags, LANES - CAP, 1), pltpu.roll(tags, LANES - 2 * CAP, 1)
    return (third - 1.0) * 65536.0 + second * 256.0 + tags


def low_of(code):
    return jnp.floor(code * (1.0 / 131072.0)) * 131072.0


def code_lines(ref, order):
    senders, depth, _ = ref.shape
    tail = depth // CAP * CAP
    per = LANES // CAP
    lines = senders // per
    lane = lax.broadcasted_iota(jnp.int32, (lines, LANES), 1)
    order[...] = codes(ref[:, tail : tail + 8, :])
    code = order[pl.ds(0, lines, stride=per), :]
    for k in range(1, per):
        turned = pltpu.roll(order[pl.ds(k, lines, stride=per), :], k * CAP, 1)
        code = jnp.where(lane >= k * CAP, turned, code)
    return code


def code_columns(ref, col_code, col_low):
    senders, depth, _ = ref.shape
    tail = depth // CAP * CAP
    tall = codes(ref[:, tail : tail + 8, :])
    tall = jnp.concatenate([tall, jnp.zeros((LANES - senders, LANES), jnp.float32)], axis=0).T
    for s in range(senders):
        col = jnp.broadcast_to(tall[:CAP, s : s + 1], (CAP, LANES))
        col_code[s * CAP : (s + 1) * CAP, :] = col
        col_low[s * CAP : (s + 1) * CAP, :] = low_of(col)


def rows_of(ref, sender, count):
    chunks = ref.shape[1] // CAP
    return jnp.concatenate(
        [
            ref[pl.ds(sender, count), j * CAP : (j + 1) * CAP, :].reshape(count * CAP, LANES)
            for j in range(chunks)
        ],
        axis=1,
    )


def reduce_tile(score, wide, row0, col_code, col_low, col_best, lanes):
    size = score.shape[0]
    step = 64
    tops = [None] * (wide // LANES)
    for r in range(0, size, step):
        rows = slice(row0 + r, row0 + r + step)
        code, low = col_code[rows, :], col_low[rows, :]
        side = None
        for c, (lane_code, lane_low, _, _, both) in enumerate(lanes):
            here = score[r : r + step, c * LANES : (c + 1) * LANES]
            here = jnp.where(low == lane_low, here, -1.0)
            less = code < lane_code
            top = jnp.max(jnp.where(less, here, -1.0).reshape(step // 8, 8, LANES), axis=0)
            tops[c] = top if tops[c] is None else jnp.maximum(tops[c], top)
            if both:
                late = jnp.where(less, -1.0, here)
                side = late if side is None else jnp.maximum(side, late)
        if side is not None:
            col_best[rows, :] = jnp.maximum(col_best[rows, :], side)
    for top, (_, _, read, write, _) in zip(tops, lanes):
        write(jnp.maximum(read(), top))


def column_maxima(col_best, row0, size):
    return [
        jnp.max(col_best[t : t + LANES, :].T, axis=0, keepdims=True)
        for t in range(row0, row0 + size, LANES)
    ]


def own_kernel(own_ref, out_ref, col_code, col_low, order, lane_code, lane_low, col_best, best, *scores):
    senders = own_ref.shape[0]
    count = senders * CAP
    size, most = scores[0].shape

    def prepare():
        code = code_lines(own_ref, order)
        low = low_of(code)
        for t in range(count // LANES):
            lane_code[:, t * LANES : (t + 1) * LANES] = code[t : t + 1]
            lane_low[:, t * LANES : (t + 1) * LANES] = low[t : t + 1]
        code_columns(own_ref, col_code, col_low)
        col_best[...] = jnp.full(col_best.shape, -1.0, jnp.float32)
        best[...] = jnp.full(best.shape, -1.0, jnp.float32)

    def reduce(at, r0, c0, wide):
        lanes = []
        for c in range(c0, c0 + wide, LANES):
            span = slice(c, c + LANES)

            def read(span=span):
                return best[:, span]

            def write(x, span=span):
                best[:, span] = x

            lanes.append((lane_code[:, span], lane_low[:, span], read, write, c >= r0 + size))
        reduce_tile(scores[at], wide, r0, col_code, col_low, col_best, lanes)

    tiles = [
        (r0, c0, min(most, count - c0)) for r0 in range(0, count, size) for c0 in range(r0, count, most)
    ]
    tops = []
    for n in range(len(tiles) + 1):
        if n < len(tiles):
            r0, c0, wide = tiles[n]
            scores[n % 2][:, :wide] = lax.dot_general(
                rows_of(own_ref, r0 // CAP, size // CAP),
                rows_of(own_ref, c0 // CAP, wide // CAP),
                NT,
                preferred_element_type=jnp.float32,
            )
        if n == 0:
            prepare()
            continue
        r0, c0, wide = tiles[n - 1]
        reduce((n - 1) % 2, r0, c0, wide)
        if c0 + wide == count:
            tops += column_maxima(col_best, r0, size)
    top = jnp.max(best[...], axis=0, keepdims=True)
    top = jnp.concatenate([top[:, t : t + LANES] for t in range(0, count, LANES)], axis=0)
    out_ref[...] = jnp.maximum(top, jnp.concatenate(tops, axis=0))


def cross_kernel(
    own_ref, other_ref, prev_ref, col_code, col_low, out_ref, order, lane_code, lane_low, col_best, best, *scores
):
    senders = own_ref.shape[0]
    count = senders * CAP
    size, most = scores[0].shape
    blocks = count // size
    each = size // LANES
    core = lax.axis_index("blk")

    def prepare():
        code = code_lines(other_ref, order)
        low = low_of(code)
        for t in range(count // LANES):
            span = slice(t % each * LANES, (t % each + 1) * LANES)
            lane_code[t // each : t // each + 1, span] = code[t : t + 1]
            lane_low[t // each : t // each + 1, span] = low[t : t + 1]
        col_best[...] = jnp.full(col_best.shape, -1.0, jnp.float32)
        best[...] = jnp.full(best.shape, -1.0, jnp.float32)

    def reduce(at, n, others):
        lanes = []
        for j in others:
            code_here, low_here = lane_code[pl.ds(j, 1), :], lane_low[pl.ds(j, 1), :]
            for c in range(0, size, LANES):
                span = slice(c, c + LANES)

                def read(j=j, span=span):
                    return best[j, :, span]

                def write(x, j=j, span=span):
                    best[j, :, span] = x

                lanes.append((code_here[:, span], low_here[:, span], read, write, True))
        reduce_tile(scores[at], len(others) * size, n * size, col_code, col_low, col_best, lanes)

    tiles = [(n, [lax.rem(n + core + k, blocks) for k in range(blocks // 2)]) for n in range(blocks)]
    tiles = tiles[:-1] + [(blocks - 1, [j]) for j in tiles[-1][1]]
    tops = []
    for t in range(len(tiles) + 1):
        if t < len(tiles):
            n, others = tiles[t]
            scores[t % 2][:, : len(others) * size] = lax.dot_general(
                rows_of(own_ref, n * size // CAP, size // CAP),
                jnp.concatenate(
                    [rows_of(other_ref, j * (size // CAP), size // CAP) for j in others], axis=0
                ),
                NT,
                preferred_element_type=jnp.float32,
            )
        if t == 0:
            prepare()
            continue
        n, others = tiles[t - 1]
        reduce((t - 1) % 2, n, others)
        if t == len(tiles) or tiles[t][0] != n:
            tops += column_maxima(col_best, n * size, size)

    per = LANES // CAP
    lines = senders // per
    mine = jnp.maximum(prev_ref[...], jnp.concatenate(tops, axis=0))
    theirs = jnp.concatenate(
        [
            jnp.max(best[t // each, :, t % each * LANES : (t % each + 1) * LANES], axis=0, keepdims=True)
            for t in range(lines)
        ],
        axis=0,
    )
    lane = lax.broadcasted_iota(jnp.int32, (lines, LANES), 1)
    for k in range(per):
        first = pltpu.roll(mine, LANES - k * CAP, 1) if k else mine
        second = pltpu.roll(theirs, (LANES + CAP - k * CAP) % LANES, 1) if k != 1 else theirs
        order[pl.ds(k, lines, stride=per), :] = jnp.where(lane < CAP, first, second)
    out_ref[...] = order[...]


def gram_call(kernel, out_shapes, operands, blocked, senders, depth, pairs):
    count = senders * CAP
    size = min(512, count)
    most = min(1024, count)
    here = pl.BlockSpec(memory_space=pltpu.VMEM)
    lanes = (count // size, size) if blocked else (1, count)
    tops = (count // size, 8, size) if blocked else (8, count)
    return pl.pallas_call(
        kernel,
        in_specs=[here] * len(operands),
        out_specs=[here] * len(out_shapes),
        out_shape=[jax.ShapeDtypeStruct(shape, jnp.float32) for shape in out_shapes],
        scratch_shapes=[
            pltpu.VMEM((senders, LANES), jnp.float32),
            pltpu.VMEM(lanes, jnp.float32),
            pltpu.VMEM(lanes, jnp.float32),
            pltpu.VMEM((count, LANES), jnp.float32),
            pltpu.VMEM(tops, jnp.float32),
            pltpu.VMEM((size, most), jnp.float32),
            pltpu.VMEM((size, most), jnp.float32),
        ],
        compiler_params=pltpu.CompilerParams(vmem_limit_bytes=24 << 20),
        cost_estimate=pl.CostEstimate(
            flops=2 * pairs * (depth // CAP) * LANES,
            bytes_accessed=4 * count * (depth // CAP) * LANES,
            transcendentals=0,
        ),
    )(*operands)


def unpack_kernel(back_ref, swap_ref, slot_ref, out_ref):
    groups = back_ref.shape[0]
    rows = slot_ref.shape[1]
    slot = slot_ref[...]
    group = lax.shift_right_logical(slot, 5)
    rank = slot & (CAP - 1)
    member = lax.broadcasted_iota(jnp.int32, (groups, rows), 0) == group
    member = jnp.where(member, 1.0, 0.0).astype(jnp.bfloat16)
    rest = jnp.maximum(back_ref[...], pltpu.roll(swap_ref[...], LANES - CAP, 1))
    found = jnp.zeros((LANES, rows), jnp.float32)
    for _ in range(3):
        piece = rest.astype(jnp.bfloat16)
        rest = rest - piece.astype(jnp.float32)
        found += lax.dot_general(
            piece, member, (((0,), (0,)), ((), ())), preferred_element_type=jnp.float32
        )
    chosen = lax.broadcasted_iota(jnp.int32, (CAP, rows), 0) == rank
    best = jnp.sum(jnp.where(chosen, found[:CAP], 0.0), axis=0, keepdims=True)
    out_ref[...] = jnp.concatenate(
        [best[:, b * LANES : (b + 1) * LANES] for b in range(rows // LANES)], axis=0
    )


def unpack(back, swap, slot):
    rows = slot.shape[1]
    return pl.pallas_call(
        unpack_kernel,
        out_shape=jax.ShapeDtypeStruct((rows // LANES, LANES), jnp.float32),
        compiler_params=pltpu.CompilerParams(vmem_limit_bytes=16 << 20),
    )(back, swap, slot)


def local(embeddings, labels, row_ids):
    groups = lax.axis_size("grp")
    rows = embeddings.shape[0]
    send, slot = pack(embeddings, labels, row_ids, groups)
    own = lax.all_to_all(send, "grp", split_axis=0, concat_axis=0, tiled=True)
    swap = [(0, 1), (1, 0)]
    other = lax.ppermute(own, "blk", swap)
    depth = own.shape[1]
    count = groups * CAP
    found, col_code, col_low = gram_call(
        own_kernel,
        [(count // LANES, LANES), (count, LANES), (count, LANES)],
        [own],
        False,
        groups,
        depth,
        count * count * 5 // 8,
    )
    [found] = gram_call(
        cross_kernel,
        [(groups, LANES)],
        [own, other, found, col_code, col_low],
        True,
        groups,
        depth,
        count * count // 2,
    )
    back = lax.all_to_all(found, "grp", split_axis=0, concat_axis=0, tiled=True)
    return unpack(back, lax.ppermute(back, "blk", swap), slot).reshape(rows)


def solution(mesh):
    in_specs = (P(("grp", "blk"), None), P(("grp", "blk")), P(("grp", "blk")))
    out_specs = P(("grp", "blk"))
    return jax.shard_map(local, mesh=mesh, in_specs=in_specs, out_specs=out_specs, check_vma=False)
```

time: 107 us -> 105 us (0.981)
  Pallas kernels: 23.4 us -> 21.6 us
    pallas_call x3, Pallas kernels: 22.4 us -> 20.6 us  [the longest x2 12.1 us: gram_call(): pl.pallas_call(kernel, in_specs=[here] * len(operands), out_specs=[here]...]
  transfers between devices with their start and end apart: 2 -> 2, of which waited for: 1 -> 2; matrix products, arithmetic and copies ran while one was open for 0% -> 0% of each run, Pallas kernels for 7% -> 6%
where the time goes in v4:
time: 105 us
  blocking collectives  78.7 us (75%)
  Pallas kernels  21.6 us (21%)
  starting transfers between devices  3.71 us (4%)
  waiting for transfers between devices  1.13 us (1%)
    all_to_all x1, blocking collectives, local(): own = lax.all_to_all(send, 'grp', split_axis=0, concat_axis=0, tiled=True)  65.2 us
    all_to_all x1, blocking collectives, local(): back = lax.all_to_all(found, 'grp', split_axis=0, concat_axis=0, tiled=True)  13.5 us
    pallas_call x2, Pallas kernels, gram_call(): pl.pallas_call(kernel, in_specs=[here] * len(operands), out_specs=[here]...  12.1 us
    pallas_call x1, Pallas kernels, pack(): pl.pallas_call(pack_kernel, in_specs=[there] * 3, out_specs=[there] * 2,...  8.5 us
  transfers between devices with their start and end apart: 2, of which 2 were waited for; matrix products, arithmetic and copies ran while one was open for 0% of the time, Pallas kernels for 6%

profile of v4, /device:TPU:1, one launch (start us, length us, event | category | flops | bytes accessed | tf_op | source)
XLA Modules:
  0.0 105.1 jit_solution(5836174430318494463)
XLA Ops:
  0.0 8.5 %shard_map.37 = (bf16[64,264,128]{2,1,0:T(8,128)(2,1)}, s32[1,1024]{1,0:T(1,128)}) custom-call(s32[8,128]{1,0:T(8,128)} %bitcast.10, s32[8,128]{1,0:T(8,128)} %bitcast.11, bf16[1024,1024]{1,0:T(8,128)(2,1)} %emb_ref.1), custom_call_target="tpu_custom_call" | custom-call | flops 4294967296 | bytes 6291456 | tf_op jit(solution)/shard_map/pallas_call | solution.py:124
  8.5 65.2 %all_to_all.16.own_ref = bf16[64,264,128]{2,1,0:T(8,128)(2,1)S(1)} all-to-all(bf16[64,264,128]{2,1,0:T(8,128)(2,1)} %get-tuple-element.10), channel_id=1, replica_groups=mesh['grp'=64,'blk'=2] {'grp'}, dimensions={0} | all-to-all | bytes 8650752 | tf_op jit(solution)/shard_map/all_to_all | solution.py:424
  73.7 1.9 %collective-permute-start = (bf16[64,264,128]{2,1,0:T(8,128)(2,1)S(1)}, bf16[64,264,128]{2,1,0:T(8,128)(2,1)S(1)}, u32[]{:S(2)}, u32[]{:S(2)}) collective-permute-start(bf16[64,264,128]{2,1,0:T(8,128)(2,1)S(1)} %all_to_all.16.own_ref), channel_id=1, source_target_pairs={{0,1},{1,0},{2,3},{3,2},{4,5},{5,4},{6,7},{7,6},{8,9},{9,8},{10,11... | collective-permute-start | bytes 12976136 | tf_op jit(solution)/shard_map/ppermute | solution.py:426
  75.6 6.7 %shard_map.38 = (f32[16,128]{1,0:T(8,128)S(1)}, f32[2048,128]{1,0:T(8,128)S(1)}, f32[2048,128]{1,0:T(8,128)S(1)}) custom-call(bf16[64,264,128]{2,1,0:T(8,128)(2,1)S(1)} %all_to_all.16.own_ref), custom_call_target="tpu_custom_call" | custom-call | flops 5368709120 | bytes 8388608 | tf_op jit(solution)/shard_map/pallas_call | solution.py:365
  82.3 0.3 collective-permute-done.other_ref
  82.6 0.0 copy-start
  82.6 5.4 %shard_map.39 = f32[64,128]{1,0:T(8,128)S(1)} custom-call(bf16[64,264,128]{2,1,0:T(8,128)(2,1)S(1)} %all_to_all.16.own_ref, bf16[64,264,128]{2,1,0:T(8,128)(2,1)S(1)} %collective-permute-done.other_ref, f32[16,128]{1,0:T(8,128)S(1)} %get-tuple-element.11.prev_ref, f32[2048,128]{1,0:T(8,128)S(1)} %get-tuple-element.12.col_code, ...), custom_call_target="tpu_custom_call" | custom-call | flops 4294967296 | bytes 8388608 | tf_op jit(solution)/shard_map/pallas_call | solution.py:365
  87.9 13.5 %all_to_all.17 = f32[64,1,128]{2,1,0:T(1,128)S(1)} all-to-all(f32[64,1,128]{2,1,0:T(1,128)S(1)} %bitcast.9), channel_id=1, replica_groups=mesh['grp'=64,'blk'=2] {'grp'}, dimensions={0} | all-to-all | bytes 65536 | tf_op jit(solution)/shard_map/all_to_all | solution.py:447
  101.4 1.8 %collective-permute-start.1 = (f32[64,128]{1,0:T(8,128)S(1)}, f32[64,128]{1,0:T(8,128)S(1)}, u32[]{:S(2)}, u32[]{:S(2)}) collective-permute-start(f32[64,128]{1,0:T(8,128)S(1)} %bitcast.7), channel_id=1, source_target_pairs={{0,1},{1,0},{2,3},{3,2},{4,5},{5,4},{6,7},{7,6},{8,9},{9,8},{10,11... | collective-permute-start | bytes 98312 | tf_op jit(solution)/shard_map/ppermute | solution.py:448
  103.2 0.9 collective-permute-done.1.swap_ref
  104.1 0.0 copy-done
  104.1 1.0 shard_map.40
Async XLA Ops:
  73.7 8.9 %collective-permute-start = (bf16[64,264,128]{2,1,0:T(8,128)(2,1)S(1)}, bf16[64,264,128]{2,1,0:T(8,128)(2,1)S(1)}, u32[]{:S(2)}, u32[]{:S(2)}) collective-permute-start(bf16[64,264,128]{2,1,0:T(8,128)(2,1)S(1)} %all_to_all.16.own_ref), channel_id=1, source_target_pairs={{0,1},{1,0},{2,3},{3,2},{4,5},{5,4},{6,7},{7,6},{8,9},{9,8},{10,11... | collective-permute-start | bytes 12976136 | tf_op jit(solution)/shard_map/ppermute | solution.py:426
  82.6 21.5 %copy-start = (s32[1,1024]{1,0:T(1,128)S(1)}, s32[1,1024]{1,0:T(1,128)}, u32[]{:S(2)}) copy-start(s32[1,1024]{1,0:T(1,128)} %get-tuple-element.14.slot_ref) | copy-start | bytes 12292
  101.4 2.7 %collective-permute-start.1 = (f32[64,128]{1,0:T(8,128)S(1)}, f32[64,128]{1,0:T(8,128)S(1)}, u32[]{:S(2)}, u32[]{:S(2)}) collective-permute-start(f32[64,128]{1,0:T(8,128)S(1)} %bitcast.7), channel_id=1, source_target_pairs={{0,1},{1,0},{2,3},{3,2},{4,5},{5,4},{6,7},{7,6},{8,9},{9,8},{10,11... | collective-permute-start | bytes 98312 | tf_op jit(solution)/shard_map/ppermute | solution.py:448

commit v5 on v4

--- a/solution.py
+++ b/solution.py
@@ -10,7 +10,7 @@
 CAP = 32
 CL_GRP = 16
 LANES = 128
-PACK_ENDS = (4, 8, 12, 14, 16)
+PACK_ENDS = (8, 13, 15, 16)
 NT = (((1,), (1,)), ((), ()))
 
 
@@ -119,7 +119,7 @@
     rows, width = embeddings.shape
     lines = rows // LANES
     depth = width // LANES * CAP + 8
-    parts, blocks = 4, len(PACK_ENDS)
+    parts, blocks = 1, len(PACK_ENDS)
     there = pl.BlockSpec(memory_space=pl.ANY)
     return pl.pallas_call(
         pack_kernel,
@@ -136,8 +136,8 @@
             pltpu.VMEM((rows, width), jnp.bfloat16),
             pltpu.VMEM((groups, depth, LANES), jnp.bfloat16),
             pltpu.VMEM((1, rows), jnp.int32),
-            pltpu.VMEM((groups // 2 * CAP, width), jnp.float32),
-            pltpu.VMEM((groups // 2 * CAP, width), jnp.float32),
+            pltpu.VMEM((groups * 3 // 4 * CAP, width), jnp.float32),
+            pltpu.VMEM((groups * 3 // 4 * CAP, width), jnp.float32),
             pltpu.SemaphoreType.DMA((parts,)),
             pltpu.SemaphoreType.DMA((blocks,)),
             pltpu.SemaphoreType.DMA((3,)),

time: 105 us -> 104 us (level)
  no operation moved by 1% of the time
where the time goes in v5:
time: 104 us
  blocking collectives  78.6 us (76%)
  Pallas kernels  20.7 us (20%)
  starting transfers between devices  3.7 us (4%)
  waiting for transfers between devices  1.13 us (1%)
    all_to_all x1, blocking collectives, local(): own = lax.all_to_all(send, 'grp', split_axis=0, concat_axis=0, tiled=True)  65.2 us
    all_to_all x1, blocking collectives, local(): back = lax.all_to_all(found, 'grp', split_axis=0, concat_axis=0, tiled=True)  13.4 us
    pallas_call x2, Pallas kernels, gram_call(): pl.pallas_call(kernel, in_specs=[here] * len(operands), out_specs=[here]...  12.1 us
    pallas_call x1, Pallas kernels, pack(): pl.pallas_call(pack_kernel, in_specs=[there] * 3, out_specs=[there] * 2,...  7.65 us
  transfers between devices with their start and end apart: 2, of which 2 were waited for; matrix products, arithmetic and copies ran while one was open for 0% of the time, Pallas kernels for 6%

profile of v5, /device:TPU:1, one launch (start us, length us, event | category | flops | bytes accessed | tf_op | source)
XLA Modules:
  0.0 104.2 jit_solution(2935007284565996421)
XLA Ops:
  0.0 7.6 %shard_map.37 = (bf16[64,264,128]{2,1,0:T(8,128)(2,1)}, s32[1,1024]{1,0:T(1,128)}) custom-call(s32[8,128]{1,0:T(8,128)} %bitcast.10, s32[8,128]{1,0:T(8,128)} %bitcast.11, bf16[1024,1024]{1,0:T(8,128)(2,1)} %emb_ref.1), custom_call_target="tpu_custom_call" | custom-call | flops 4294967296 | bytes 6291456 | tf_op jit(solution)/shard_map/pallas_call | solution.py:124
  7.7 65.2 %all_to_all.16.own_ref = bf16[64,264,128]{2,1,0:T(8,128)(2,1)S(1)} all-to-all(bf16[64,264,128]{2,1,0:T(8,128)(2,1)} %get-tuple-element.10), channel_id=1, replica_groups=mesh['grp'=64,'blk'=2] {'grp'}, dimensions={0} | all-to-all | bytes 8650752 | tf_op jit(solution)/shard_map/all_to_all | solution.py:424
  72.9 1.9 %collective-permute-start = (bf16[64,264,128]{2,1,0:T(8,128)(2,1)S(1)}, bf16[64,264,128]{2,1,0:T(8,128)(2,1)S(1)}, u32[]{:S(2)}, u32[]{:S(2)}) collective-permute-start(bf16[64,264,128]{2,1,0:T(8,128)(2,1)S(1)} %all_to_all.16.own_ref), channel_id=1, source_target_pairs={{0,1},{1,0},{2,3},{3,2},{4,5},{5,4},{6,7},{7,6},{8,9},{9,8},{10,11... | collective-permute-start | bytes 12976136 | tf_op jit(solution)/shard_map/ppermute | solution.py:426
  74.7 6.7 %shard_map.38 = (f32[16,128]{1,0:T(8,128)S(1)}, f32[2048,128]{1,0:T(8,128)S(1)}, f32[2048,128]{1,0:T(8,128)S(1)}) custom-call(bf16[64,264,128]{2,1,0:T(8,128)(2,1)S(1)} %all_to_all.16.own_ref), custom_call_target="tpu_custom_call" | custom-call | flops 5368709120 | bytes 8388608 | tf_op jit(solution)/shard_map/pallas_call | solution.py:365
  81.4 0.3 collective-permute-done.other_ref
  81.7 0.0 copy-start
  81.7 5.4 %shard_map.39 = f32[64,128]{1,0:T(8,128)S(1)} custom-call(bf16[64,264,128]{2,1,0:T(8,128)(2,1)S(1)} %all_to_all.16.own_ref, bf16[64,264,128]{2,1,0:T(8,128)(2,1)S(1)} %collective-permute-done.other_ref, f32[16,128]{1,0:T(8,128)S(1)} %get-tuple-element.11.prev_ref, f32[2048,128]{1,0:T(8,128)S(1)} %get-tuple-element.12.col_code, ...), custom_call_target="tpu_custom_call" | custom-call | flops 4294967296 | bytes 8388608 | tf_op jit(solution)/shard_map/pallas_call | solution.py:365
  87.1 13.4 %all_to_all.17 = f32[64,1,128]{2,1,0:T(1,128)S(1)} all-to-all(f32[64,1,128]{2,1,0:T(1,128)S(1)} %bitcast.9), channel_id=1, replica_groups=mesh['grp'=64,'blk'=2] {'grp'}, dimensions={0} | all-to-all | bytes 65536 | tf_op jit(solution)/shard_map/all_to_all | solution.py:447
  100.5 1.8 %collective-permute-start.1 = (f32[64,128]{1,0:T(8,128)S(1)}, f32[64,128]{1,0:T(8,128)S(1)}, u32[]{:S(2)}, u32[]{:S(2)}) collective-permute-start(f32[64,128]{1,0:T(8,128)S(1)} %bitcast.7), channel_id=1, source_target_pairs={{0,1},{1,0},{2,3},{3,2},{4,5},{5,4},{6,7},{7,6},{8,9},{9,8},{10,11... | collective-permute-start | bytes 98312 | tf_op jit(solution)/shard_map/ppermute | solution.py:448
  102.3 0.9 collective-permute-done.1.swap_ref
  103.2 0.0 copy-done
  103.2 1.0 shard_map.40
Async XLA Ops:
  72.9 8.9 %collective-permute-start = (bf16[64,264,128]{2,1,0:T(8,128)(2,1)S(1)}, bf16[64,264,128]{2,1,0:T(8,128)(2,1)S(1)}, u32[]{:S(2)}, u32[]{:S(2)}) collective-permute-start(bf16[64,264,128]{2,1,0:T(8,128)(2,1)S(1)} %all_to_all.16.own_ref), channel_id=1, source_target_pairs={{0,1},{1,0},{2,3},{3,2},{4,5},{5,4},{6,7},{7,6},{8,9},{9,8},{10,11... | collective-permute-start | bytes 12976136 | tf_op jit(solution)/shard_map/ppermute | solution.py:426
  81.7 21.5 %copy-start = (s32[1,1024]{1,0:T(1,128)S(1)}, s32[1,1024]{1,0:T(1,128)}, u32[]{:S(2)}) copy-start(s32[1,1024]{1,0:T(1,128)} %get-tuple-element.14.slot_ref) | copy-start | bytes 12292
  100.5 2.7 %collective-permute-start.1 = (f32[64,128]{1,0:T(8,128)S(1)}, f32[64,128]{1,0:T(8,128)S(1)}, u32[]{:S(2)}, u32[]{:S(2)}) collective-permute-start(f32[64,128]{1,0:T(8,128)S(1)} %bitcast.7), channel_id=1, source_target_pairs={{0,1},{1,0},{2,3},{3,2},{4,5},{5,4},{6,7},{7,6},{8,9},{9,8},{10,11... | collective-permute-start | bytes 98312 | tf_op jit(solution)/shard_map/ppermute | solution.py:448

commit v6 on v5

--- a/solution.py
+++ b/solution.py
@@ -43,6 +43,7 @@
         load(p).start()
 
     fetch_labels.wait()
+    fetch_ids.wait()
     labels = lab[...]
     place = (
         lax.broadcasted_iota(jnp.int32, (lines, LANES), 0) * LANES
@@ -65,9 +66,7 @@
     group = flat(target)
     slot = group * CAP + rank
     slots[...] = slot
-    keep_slots.start()
-
-    fetch_ids.wait()
+
     ids = num[...]
     pieces = [
         ids & 255,
@@ -101,6 +100,8 @@
                 :, j * LANES : (j + 1) * LANES
             ].reshape(end - at, CAP, LANES)
         store(n).start()
+        if n == 0:
+            keep_slots.start()
 
     for n, (at, end) in enumerate(spans):
         size = (end - at) * CAP
@@ -393,8 +394,8 @@
     rank = slot & (CAP - 1)
     member = lax.broadcasted_iota(jnp.int32, (groups, rows), 0) == group
     member = jnp.where(member, 1.0, 0.0).astype(jnp.bfloat16)
-    rest = jnp.maximum(back_ref[...], pltpu.roll(swap_ref[...], LANES - CAP, 1))
-    found = jnp.zeros((LANES, rows), jnp.float32)
+    rest = jnp.maximum(back_ref[...], pltpu.roll(swap_ref[...], LANES - CAP, 1))[:, :CAP]
+    found = jnp.zeros((CAP, rows), jnp.float32)
     for _ in range(3):
         piece = rest.astype(jnp.bfloat16)
         rest = rest - piece.astype(jnp.float32)
@@ -402,7 +403,7 @@
             piece, member, (((0,), (0,)), ((), ())), preferred_element_type=jnp.float32
         )
     chosen = lax.broadcasted_iota(jnp.int32, (CAP, rows), 0) == rank
-    best = jnp.sum(jnp.where(chosen, found[:CAP], 0.0), axis=0, keepdims=True)
+    best = jnp.sum(jnp.where(chosen, found, 0.0), axis=0, keepdims=True)
     out_ref[...] = jnp.concatenate(
         [best[:, b * LANES : (b + 1) * LANES] for b in range(rows // LANES)], axis=0
     )

time: 104 us -> 104 us (level)
  no operation moved by 1% of the time
where the time goes in v6:
time: 104 us
  blocking collectives  78.6 us (76%)
  Pallas kernels  20.3 us (20%)
  starting transfers between devices  3.7 us (4%)
  waiting for transfers between devices  1.13 us (1%)
    all_to_all x1, blocking collectives, local(): own = lax.all_to_all(send, 'grp', split_axis=0, concat_axis=0, tiled=True)  65.2 us
    all_to_all x1, blocking collectives, local(): back = lax.all_to_all(found, 'grp', split_axis=0, concat_axis=0, tiled=True)  13.4 us
    pallas_call x2, Pallas kernels, gram_call(): pl.pallas_call(kernel, in_specs=[here] * len(operands), out_specs=[here]...  12.1 us
    pallas_call x1, Pallas kernels, pack(): pl.pallas_call(pack_kernel, in_specs=[there] * 3, out_specs=[there] * 2,...  7.36 us
  transfers between devices with their start and end apart: 2, of which 2 were waited for; matrix products, arithmetic and copies ran while one was open for 0% of the time, Pallas kernels for 6%

profile of v6, /device:TPU:1, one launch (start us, length us, event | category | flops | bytes accessed | tf_op | source)
XLA Modules:
  0.0 103.8 jit_solution(5193144654713744373)
XLA Ops:
  0.0 7.4 %shard_map.37 = (bf16[64,264,128]{2,1,0:T(8,128)(2,1)}, s32[1,1024]{1,0:T(1,128)}) custom-call(s32[8,128]{1,0:T(8,128)} %bitcast.10, s32[8,128]{1,0:T(8,128)} %bitcast.11, bf16[1024,1024]{1,0:T(8,128)(2,1)} %emb_ref.1), custom_call_target="tpu_custom_call" | custom-call | flops 4294967296 | bytes 6291456 | tf_op jit(solution)/shard_map/pallas_call | solution.py:125
  7.4 65.2 %all_to_all.16.own_ref = bf16[64,264,128]{2,1,0:T(8,128)(2,1)S(1)} all-to-all(bf16[64,264,128]{2,1,0:T(8,128)(2,1)} %get-tuple-element.10), channel_id=1, replica_groups=mesh['grp'=64,'blk'=2] {'grp'}, dimensions={0} | all-to-all | bytes 8650752 | tf_op jit(solution)/shard_map/all_to_all | solution.py:425
  72.6 1.9 %collective-permute-start = (bf16[64,264,128]{2,1,0:T(8,128)(2,1)S(1)}, bf16[64,264,128]{2,1,0:T(8,128)(2,1)S(1)}, u32[]{:S(2)}, u32[]{:S(2)}) collective-permute-start(bf16[64,264,128]{2,1,0:T(8,128)(2,1)S(1)} %all_to_all.16.own_ref), channel_id=1, source_target_pairs={{0,1},{1,0},{2,3},{3,2},{4,5},{5,4},{6,7},{7,6},{8,9},{9,8},{10,11... | collective-permute-start | bytes 12976136 | tf_op jit(solution)/shard_map/ppermute | solution.py:427
  74.5 6.7 %shard_map.38 = (f32[16,128]{1,0:T(8,128)S(1)}, f32[2048,128]{1,0:T(8,128)S(1)}, f32[2048,128]{1,0:T(8,128)S(1)}) custom-call(bf16[64,264,128]{2,1,0:T(8,128)(2,1)S(1)} %all_to_all.16.own_ref), custom_call_target="tpu_custom_call" | custom-call | flops 5368709120 | bytes 8388608 | tf_op jit(solution)/shard_map/pallas_call | solution.py:366
  81.2 0.3 collective-permute-done.other_ref
  81.4 0.0 copy-start
  81.4 5.4 %shard_map.39 = f32[64,128]{1,0:T(8,128)S(1)} custom-call(bf16[64,264,128]{2,1,0:T(8,128)(2,1)S(1)} %all_to_all.16.own_ref, bf16[64,264,128]{2,1,0:T(8,128)(2,1)S(1)} %collective-permute-done.other_ref, f32[16,128]{1,0:T(8,128)S(1)} %get-tuple-element.11.prev_ref, f32[2048,128]{1,0:T(8,128)S(1)} %get-tuple-element.12.col_code, ...), custom_call_target="tpu_custom_call" | custom-call | flops 4294967296 | bytes 8388608 | tf_op jit(solution)/shard_map/pallas_call | solution.py:366
  86.8 13.4 %all_to_all.17 = f32[64,1,128]{2,1,0:T(1,128)S(1)} all-to-all(f32[64,1,128]{2,1,0:T(1,128)S(1)} %bitcast.9), channel_id=1, replica_groups=mesh['grp'=64,'blk'=2] {'grp'}, dimensions={0} | all-to-all | bytes 65536 | tf_op jit(solution)/shard_map/all_to_all | solution.py:448
  100.2 1.8 %collective-permute-start.1 = (f32[64,128]{1,0:T(8,128)S(1)}, f32[64,128]{1,0:T(8,128)S(1)}, u32[]{:S(2)}, u32[]{:S(2)}) collective-permute-start(f32[64,128]{1,0:T(8,128)S(1)} %bitcast.7), channel_id=1, source_target_pairs={{0,1},{1,0},{2,3},{3,2},{4,5},{5,4},{6,7},{7,6},{8,9},{9,8},{10,11... | collective-permute-start | bytes 98312 | tf_op jit(solution)/shard_map/ppermute | solution.py:449
  102.1 0.9 collective-permute-done.1.swap_ref
  102.9 0.0 copy-done
  102.9 0.9 shard_map.40
Async XLA Ops:
  72.6 8.9 %collective-permute-start = (bf16[64,264,128]{2,1,0:T(8,128)(2,1)S(1)}, bf16[64,264,128]{2,1,0:T(8,128)(2,1)S(1)}, u32[]{:S(2)}, u32[]{:S(2)}) collective-permute-start(bf16[64,264,128]{2,1,0:T(8,128)(2,1)S(1)} %all_to_all.16.own_ref), channel_id=1, source_target_pairs={{0,1},{1,0},{2,3},{3,2},{4,5},{5,4},{6,7},{7,6},{8,9},{9,8},{10,11... | collective-permute-start | bytes 12976136 | tf_op jit(solution)/shard_map/ppermute | solution.py:427
  81.4 21.5 %copy-start = (s32[1,1024]{1,0:T(1,128)S(1)}, s32[1,1024]{1,0:T(1,128)}, u32[]{:S(2)}) copy-start(s32[1,1024]{1,0:T(1,128)} %get-tuple-element.14.slot_ref) | copy-start | bytes 12292
  100.2 2.7 %collective-permute-start.1 = (f32[64,128]{1,0:T(8,128)S(1)}, f32[64,128]{1,0:T(8,128)S(1)}, u32[]{:S(2)}, u32[]{:S(2)}) collective-permute-start(f32[64,128]{1,0:T(8,128)S(1)} %bitcast.7), channel_id=1, source_target_pairs={{0,1},{1,0},{2,3},{3,2},{4,5},{5,4},{6,7},{7,6},{8,9},{9,8},{10,11... | collective-permute-start | bytes 98312 | tf_op jit(solution)/shard_map/ppermute | solution.py:449

commit v7 on v6

--- a/solution.py
+++ b/solution.py
@@ -300,7 +300,7 @@
         col_best[...] = jnp.full(col_best.shape, -1.0, jnp.float32)
         best[...] = jnp.full(best.shape, -1.0, jnp.float32)
 
-    def reduce(at, n, others):
+    def reduce(at, row0, rows, others):
         lanes = []
         for j in others:
             code_here, low_here = lane_code[pl.ds(j, 1), :], lane_low[pl.ds(j, 1), :]
@@ -314,29 +314,33 @@
                     best[j, :, span] = x
 
                 lanes.append((code_here[:, span], low_here[:, span], read, write, True))
-        reduce_tile(scores[at], len(others) * size, n * size, col_code, col_low, col_best, lanes)
-
-    tiles = [(n, [lax.rem(n + core + k, blocks) for k in range(blocks // 2)]) for n in range(blocks)]
-    tiles = tiles[:-1] + [(blocks - 1, [j]) for j in tiles[-1][1]]
+        reduce_tile(scores[at].at[:rows], len(others) * size, row0, col_code, col_low, col_best, lanes)
+
+    half = blocks // 2
+    tiles = []
+    for n in range(half):
+        j = lax.rem(n + core, half)
+        cut = [size, size] if n < half - 1 else [size, size // 2, size // 2]
+        at = n * 2 * size
+        for rows in cut:
+            tiles.append((at, rows, j))
+            at += rows
     tops = []
     for t in range(len(tiles) + 1):
         if t < len(tiles):
-            n, others = tiles[t]
-            scores[t % 2][:, : len(others) * size] = lax.dot_general(
-                rows_of(own_ref, n * size // CAP, size // CAP),
-                jnp.concatenate(
-                    [rows_of(other_ref, j * (size // CAP), size // CAP) for j in others], axis=0
-                ),
+            at, rows, j = tiles[t]
+            scores[t % 2][:rows] = lax.dot_general(
+                rows_of(own_ref, at // CAP, rows // CAP),
+                rows_of(other_ref, j * (2 * size // CAP), 2 * size // CAP),
                 NT,
                 preferred_element_type=jnp.float32,
             )
         if t == 0:
             prepare()
             continue
-        n, others = tiles[t - 1]
-        reduce((t - 1) % 2, n, others)
-        if t == len(tiles) or tiles[t][0] != n:
-            tops += column_maxima(col_best, n * size, size)
+        at, rows, j = tiles[t - 1]
+        reduce((t - 1) % 2, at, rows, [j * 2, j * 2 + 1])
+        tops += column_maxima(col_best, at, rows)
 
     per = LANES // CAP
     lines = senders // per

time: 104 us -> 104 us (level)
  no operation moved by 1% of the time
where the time goes in v7:
time: 104 us
  blocking collectives  78.7 us (76%)
  Pallas kernels  20.3 us (20%)
  starting transfers between devices  3.69 us (4%)
  waiting for transfers between devices  1.13 us (1%)
    all_to_all x1, blocking collectives, local(): own = lax.all_to_all(send, 'grp', split_axis=0, concat_axis=0, tiled=True)  65.2 us
    all_to_all x1, blocking collectives, local(): back = lax.all_to_all(found, 'grp', split_axis=0, concat_axis=0, tiled=True)  13.5 us
    pallas_call x2, Pallas kernels, gram_call(): pl.pallas_call(kernel, in_specs=[here] * len(operands), out_specs=[here]...  12 us
    pallas_call x1, Pallas kernels, pack(): pl.pallas_call(pack_kernel, in_specs=[there] * 3, out_specs=[there] * 2,...  7.36 us
  transfers between devices with their start and end apart: 2, of which 2 were waited for; matrix products, arithmetic and copies ran while one was open for 0% of the time, Pallas kernels for 6%

profile of v7, /device:TPU:1, one launch (start us, length us, event | category | flops | bytes accessed | tf_op | source)
XLA Modules:
  0.0 103.8 jit_solution(14464450336502945348)
XLA Ops:
  0.0 7.4 %shard_map.37 = (bf16[64,264,128]{2,1,0:T(8,128)(2,1)}, s32[1,1024]{1,0:T(1,128)}) custom-call(s32[8,128]{1,0:T(8,128)} %bitcast.10, s32[8,128]{1,0:T(8,128)} %bitcast.11, bf16[1024,1024]{1,0:T(8,128)(2,1)} %emb_ref.1), custom_call_target="tpu_custom_call" | custom-call | flops 4294967296 | bytes 6291456 | tf_op jit(solution)/shard_map/pallas_call | solution.py:125
  7.4 65.2 %all_to_all.16.own_ref = bf16[64,264,128]{2,1,0:T(8,128)(2,1)S(1)} all-to-all(bf16[64,264,128]{2,1,0:T(8,128)(2,1)} %get-tuple-element.10), channel_id=1, replica_groups=mesh['grp'=64,'blk'=2] {'grp'}, dimensions={0} | all-to-all | bytes 8650752 | tf_op jit(solution)/shard_map/all_to_all | solution.py:429
  72.6 1.9 %collective-permute-start = (bf16[64,264,128]{2,1,0:T(8,128)(2,1)S(1)}, bf16[64,264,128]{2,1,0:T(8,128)(2,1)S(1)}, u32[]{:S(2)}, u32[]{:S(2)}) collective-permute-start(bf16[64,264,128]{2,1,0:T(8,128)(2,1)S(1)} %all_to_all.16.own_ref), channel_id=1, source_target_pairs={{0,1},{1,0},{2,3},{3,2},{4,5},{5,4},{6,7},{7,6},{8,9},{9,8},{10,11... | collective-permute-start | bytes 12976136 | tf_op jit(solution)/shard_map/ppermute | solution.py:431
  74.5 6.7 %shard_map.38 = (f32[16,128]{1,0:T(8,128)S(1)}, f32[2048,128]{1,0:T(8,128)S(1)}, f32[2048,128]{1,0:T(8,128)S(1)}) custom-call(bf16[64,264,128]{2,1,0:T(8,128)(2,1)S(1)} %all_to_all.16.own_ref), custom_call_target="tpu_custom_call" | custom-call | flops 5368709120 | bytes 8388608 | tf_op jit(solution)/shard_map/pallas_call | solution.py:370
  81.2 0.3 collective-permute-done.other_ref
  81.4 0.0 copy-start
  81.4 5.3 %shard_map.39 = f32[64,128]{1,0:T(8,128)S(1)} custom-call(bf16[64,264,128]{2,1,0:T(8,128)(2,1)S(1)} %all_to_all.16.own_ref, bf16[64,264,128]{2,1,0:T(8,128)(2,1)S(1)} %collective-permute-done.other_ref, f32[16,128]{1,0:T(8,128)S(1)} %get-tuple-element.11.prev_ref, f32[2048,128]{1,0:T(8,128)S(1)} %get-tuple-element.12.col_code, ...), custom_call_target="tpu_custom_call" | custom-call | flops 4294967296 | bytes 8388608 | tf_op jit(solution)/shard_map/pallas_call | solution.py:370
  86.8 13.5 %all_to_all.17 = f32[64,1,128]{2,1,0:T(1,128)S(1)} all-to-all(f32[64,1,128]{2,1,0:T(1,128)S(1)} %bitcast.9), channel_id=1, replica_groups=mesh['grp'=64,'blk'=2] {'grp'}, dimensions={0} | all-to-all | bytes 65536 | tf_op jit(solution)/shard_map/all_to_all | solution.py:452
  100.2 1.8 %collective-permute-start.1 = (f32[64,128]{1,0:T(8,128)S(1)}, f32[64,128]{1,0:T(8,128)S(1)}, u32[]{:S(2)}, u32[]{:S(2)}) collective-permute-start(f32[64,128]{1,0:T(8,128)S(1)} %bitcast.7), channel_id=1, source_target_pairs={{0,1},{1,0},{2,3},{3,2},{4,5},{5,4},{6,7},{7,6},{8,9},{9,8},{10,11... | collective-permute-start | bytes 98312 | tf_op jit(solution)/shard_map/ppermute | solution.py:453
  102.0 0.9 collective-permute-done.1.swap_ref
  102.9 0.0 copy-done
  102.9 0.9 shard_map.40
Async XLA Ops:
  72.6 8.9 %collective-permute-start = (bf16[64,264,128]{2,1,0:T(8,128)(2,1)S(1)}, bf16[64,264,128]{2,1,0:T(8,128)(2,1)S(1)}, u32[]{:S(2)}, u32[]{:S(2)}) collective-permute-start(bf16[64,264,128]{2,1,0:T(8,128)(2,1)S(1)} %all_to_all.16.own_ref), channel_id=1, source_target_pairs={{0,1},{1,0},{2,3},{3,2},{4,5},{5,4},{6,7},{7,6},{8,9},{9,8},{10,11... | collective-permute-start | bytes 12976136 | tf_op jit(solution)/shard_map/ppermute | solution.py:431
  81.4 21.5 %copy-start = (s32[1,1024]{1,0:T(1,128)S(1)}, s32[1,1024]{1,0:T(1,128)}, u32[]{:S(2)}) copy-start(s32[1,1024]{1,0:T(1,128)} %get-tuple-element.14.slot_ref) | copy-start | bytes 12292
  100.2 2.7 %collective-permute-start.1 = (f32[64,128]{1,0:T(8,128)S(1)}, f32[64,128]{1,0:T(8,128)S(1)}, u32[]{:S(2)}, u32[]{:S(2)}) collective-permute-start(f32[64,128]{1,0:T(8,128)S(1)} %bitcast.7), channel_id=1, source_target_pairs={{0,1},{1,0},{2,3},{3,2},{4,5},{5,4},{6,7},{7,6},{8,9},{9,8},{10,11... | collective-permute-start | bytes 98312 | tf_op jit(solution)/shard_map/ppermute | solution.py:453
